TPU v7x, 32 devices: a whole 2x2x4 slice. The times are simulated.
32 devices in a mesh: grp: 8 (over y, x, core), dp: 4 (over z).
Axes of the slice: x: 2, y: 2, z: 4, core: 2. Of those that a mesh axis runs over, the one named last changes fastest.
Arguments:
- tokens: bfloat16 [32, 1024, 1024], P(('grp', 'dp')), may hold values from -6 to 6
- out_cotangent: bfloat16 [32, 1024, 1024], P(('grp', 'dp')), may hold values from -6 to 6
- lengths: int32 [32], replicated, may hold values from 256 to 1024, as said below
- places: int32 [32, 64], replicated, may hold values from 0 to 255, as said below
- deal: int32 [32], replicated, may hold values from 0 to 31, each once
- in_weights: float32 [6, 1024, 1024], P(None, 'grp', 'dp'), may hold values from -0.1875 to 0.1875
- out_weight: float32 [1024, 1024], P('grp', 'dp'), may hold values from -4 to 4
- up_weight: float32 [1024, 4096], P('grp', 'dp'), may hold values from -0.1875 to 0.1875
- down_weight: float32 [4096, 1024], P('grp', 'dp'), may hold values from -0.09375 to 0.09375
- vectors: float32 [14, 1024], P(None, 'dp')
- first_in: float32 [6, 1024, 1024], P(None, 'grp', 'dp'), may hold values from -6 to 6
- first_out: float32 [1024, 1024], P('grp', 'dp'), may hold values from -6 to 6
- first_up: float32 [1024, 4096], P('grp', 'dp'), may hold values from -6 to 6
- first_down: float32 [4096, 1024], P('grp', 'dp'), may hold values from -6 to 6
- first_vectors: float32 [14, 1024], P(None, 'dp'), may hold values from -180 to 180
- second_in: float32 [6, 1024, 1024], P(None, 'grp', 'dp'), may hold values from 1 to 100
- second_out: float32 [1024, 1024], P('grp', 'dp'), may hold values from 0.01 to 1
- second_up: float32 [1024, 4096], P('grp', 'dp'), may hold values from 1 to 100
- second_down: float32 [4096, 1024], P('grp', 'dp'), may hold values from 1 to 100
- second_vectors: float32 [14, 1024], P(None, 'dp'), may hold values from 1 to 100
Outputs:
- layer_out: bfloat16 [32, 1024, 1024], P(('grp', 'dp'))
- token_gradient: bfloat16 [32, 1024, 1024], P(('grp', 'dp'))
- update_in: float32 [6, 1024, 1024], P(None, 'grp', 'dp')
- update_out: float32 [1024, 1024], P('grp', 'dp')
- update_up: float32 [1024, 4096], P('grp', 'dp')
- update_down: float32 [4096, 1024], P('grp', 'dp')
- update_vectors: float32 [14, 1024], P(None, 'dp')
- moment_in: float32 [6, 1024, 1024], P(None, 'grp', 'dp')
- moment_out: float32 [1024, 1024], P('grp', 'dp')
- moment_up: float32 [1024, 4096], P('grp', 'dp')
- moment_down: float32 [4096, 1024], P('grp', 'dp')
- moment_vectors: float32 [14, 1024], P(None, 'dp')
- square_in: float32 [6, 1024, 1024], P(None, 'grp', 'dp')
- square_out: float32 [1024, 1024], P('grp', 'dp')
- square_up: float32 [1024, 4096], P('grp', 'dp')
- square_down: float32 [4096, 1024], P('grp', 'dp')
- square_vectors: float32 [14, 1024], P(None, 'dp')
Inputs may be any that keep to these rules, and one draw needn't show every extreme that they name: `lengths`: one sequence has exactly 1024 tokens; every length is 256 or more. `places`: each row holds 64 distinct increasing positions below 256, hence below that sequence's length. Sequence s is computed by the device of index deal[s] along grp+dp.
All inputs are finite; a program needn't handle non-finite values.
Results may differ from a plain program's by a relative error of at most 0.02.
Values may be sent and summed in bfloat16 or wider, within the bound.
A program may use at most 448 MiB of HBM per device.

v0:
```python
import jax
import jax.numpy as jnp
from jax import lax
from jax.sharding import PartitionSpec as P

D = 1024
H = 16
HD = 64
FF = 4096
W = 512
NG = 64
STEP = 10


EPS_NORM = 1e-05
WEIGHT_DECAY = 0.1
BETA_FIRST = 0.5
BETA_SECOND = 0.999
EPS_ADAM = 1e-08
NEGATIVE = -1e30


def norm_rows(mixture):
    centered = mixture - jnp.mean(mixture, axis=-1, keepdims=True)
    variance = jnp.mean(centered * centered, axis=-1, keepdims=True)
    return centered * lax.rsqrt(variance + EPS_NORM)


def post_norm(mixture, scaling, offset):
    return norm_rows(mixture) * scaling + offset


def gelu_exact(before):
    return jax.nn.gelu(before, approximate=False)


def product(left_side, right_side):
    return jnp.dot(left_side, right_side, preferred_element_type=jnp.float32)


def product_back(left_side, right_side):
    return lax.dot_general(
        left_side, right_side, (((1,), (1,)), ((), ())), preferred_element_type=jnp.float32
    )


def product_left(left_side, right_side):
    return lax.dot_general(
        left_side, right_side, (((0,), (0,)), ((), ())), preferred_element_type=jnp.float32
    )


def split_heads(matrix):
    return matrix.reshape(matrix.shape[0], H, HD)


def column_sums(matrix):
    return jnp.sum(matrix.astype(jnp.float32), axis=0)


def adam_update(weight, gradient, moment, square, decay_rate, fix_first, fix_second):
    moment_new = BETA_FIRST * moment + (1.0 - BETA_FIRST) * gradient
    square_new = BETA_SECOND * square + (1.0 - BETA_SECOND) * gradient * gradient
    update = moment_new / fix_first / (jnp.sqrt(square_new / fix_second) + EPS_ADAM)
    return (update + decay_rate * weight, moment_new, square_new)


def per_device(
    tokens,
    out_cotangent,
    lengths,
    places,
    deal,
    in_weights,
    out_weight,
    up_weight,
    down_weight,
    vectors,
    first_in,
    first_out,
    first_up,
    first_down,
    first_vectors,
    second_in,
    second_out,
    second_up,
    second_down,
    second_vectors,
):
    inverse = jnp.argsort(deal)
    own_sequence = inverse[lax.axis_index(("grp", "dp"))]
    length = lengths[own_sequence]
    spots = places[own_sequence]
    spread_rows = lax.all_to_all(tokens, ("grp", "dp"), split_axis=1, concat_axis=0, tiled=True)
    spread_rows = jnp.take(spread_rows, inverse, axis=0)
    sequence = lax.all_to_all(spread_rows, ("grp", "dp"), split_axis=0, concat_axis=1, tiled=True)[
        0
    ]
    low_in = in_weights.astype(jnp.bfloat16)
    low_out = out_weight.astype(jnp.bfloat16)
    low_up = up_weight.astype(jnp.bfloat16)
    low_down = down_weight.astype(jnp.bfloat16)
    low_vectors = vectors.astype(jnp.bfloat16)
    inner_in, inner_out, inner_up, inner_down, full_vectors = (
        lax.all_gather(low_in, "dp", axis=2, tiled=True),
        lax.all_gather(low_out, "dp", axis=1, tiled=True),
        lax.all_gather(low_up, "dp", axis=1, tiled=True),
        lax.all_gather(low_down, "dp", axis=1, tiled=True),
        lax.all_gather(low_vectors, "dp", axis=1, tiled=True),
    )
    full_in, full_out, full_up, full_down = (
        lax.all_gather(inner_in, "grp", axis=1, tiled=True),
        lax.all_gather(inner_out, "grp", axis=0, tiled=True),
        lax.all_gather(inner_up, "grp", axis=0, tiled=True),
        lax.all_gather(inner_down, "grp", axis=0, tiled=True),
    )
    extra = FF // D
    vector_rows = full_vectors.astype(jnp.float32)
    span = sequence.shape[0]
    positions = jnp.arange(span, dtype=jnp.int32)
    global_row = jnp.any(positions[:, None] == spots[None, :], axis=1)
    key_valid = positions < length
    valid_column = key_valid[:, None].astype(jnp.float32)
    scale = HD ** (-0.5)
    half = W // 2
    block_rows = min(512, span)
    slab_rows = block_rows + 2 * half
    query = (product(sequence, full_in[0]) + vector_rows[0]).astype(jnp.bfloat16)
    keys_local = product(sequence, full_in[1]).astype(jnp.bfloat16)
    values_local = (product(sequence, full_in[2]) + vector_rows[1]).astype(jnp.bfloat16)
    rows_global = jnp.take(sequence, spots, axis=0)
    query_global = (product(rows_global, full_in[3]) + vector_rows[3]).astype(jnp.bfloat16)
    keys_global = product(sequence, full_in[4]).astype(jnp.bfloat16)
    values_global = (product(sequence, full_in[5]) + vector_rows[4]).astype(jnp.bfloat16)
    keys_padded = jnp.pad(keys_local, ((half, half), (0, 0)))
    values_padded = jnp.pad(values_local, ((half, half), (0, 0)))
    slab_valid = jnp.pad(key_valid & jnp.logical_not(global_row), (half, half))
    keys_spot = split_heads(jnp.take(keys_local, spots, axis=0))
    values_spot = split_heads(jnp.take(values_local, spots, axis=0))
    query_heads = split_heads(query)

    def block_scores(start):
        query_block = query_heads[start : start + block_rows]
        keys_slab = split_heads(keys_padded[start : start + slab_rows])
        raw_local = (
            jnp.einsum("ihd,jhd->hij", query_block, keys_slab, preferred_element_type=jnp.float32)
            * scale
        )
        raw_spot = (
            jnp.einsum("ihd,jhd->hij", query_block, keys_spot, preferred_element_type=jnp.float32)
            * scale
        )
        rows_at = start + jnp.arange(block_rows)
        cols_at = start - half + jnp.arange(slab_rows)
        allowed = (jnp.abs(rows_at[:, None] - cols_at[None, :]) <= half) & slab_valid[
            start : start + slab_rows
        ][None, :]
        return (jnp.where(allowed[None], raw_local, NEGATIVE), raw_spot, allowed[None])

    outputs_local = []
    log_sums = []
    for index_block in range(span // block_rows):
        start = index_block * block_rows
        masked, raw_spot, allowed = block_scores(start)
        top_score = jnp.maximum(jnp.max(masked, axis=-1), jnp.max(raw_spot, axis=-1))[..., None]
        total = jnp.sum(
            jnp.where(allowed, jnp.exp(masked - top_score), 0.0), axis=-1, keepdims=True
        )
        total = total + jnp.sum(jnp.exp(raw_spot - top_score), axis=-1, keepdims=True)
        log_sum = top_score + jnp.log(total)
        weights_local = jnp.where(allowed, jnp.exp(masked - log_sum), 0.0).astype(jnp.bfloat16)
        weights_spot = jnp.exp(raw_spot - log_sum).astype(jnp.bfloat16)
        values_slab = split_heads(values_padded[start : start + slab_rows])
        mixed = jnp.einsum(
            "hij,jhd->ihd", weights_local, values_slab, preferred_element_type=jnp.float32
        )
        mixed = mixed + jnp.einsum(
            "hij,jhd->ihd", weights_spot, values_spot, preferred_element_type=jnp.float32
        )
        outputs_local.append(mixed.reshape(block_rows, D))
        log_sums.append(log_sum)
    raw_global = (
        jnp.einsum(
            "ghd,jhd->hgj",
            split_heads(query_global),
            split_heads(keys_global),
            preferred_element_type=jnp.float32,
        )
        * scale
    )
    global_probs = jax.nn.softmax(
        jnp.where(key_valid[None, None, :], raw_global, NEGATIVE), axis=-1
    )
    global_low = global_probs.astype(jnp.bfloat16)
    global_out = jnp.einsum(
        "hgj,jhd->ghd", global_low, split_heads(values_global), preferred_element_type=jnp.float32
    ).reshape(NG, D)
    attended = jnp.concatenate(outputs_local, axis=0).at[spots].set(global_out).astype(jnp.bfloat16)
    branch = product(attended, full_out) + vector_rows[2]
    mixture = sequence.astype(jnp.float32) + branch
    first_norm, norm_one_back = jax.vjp(
        post_norm, mixture, vector_rows[6 + extra], vector_rows[7 + extra]
    )
    first_low = first_norm.astype(jnp.bfloat16)
    hidden_pre = product(first_low, full_up) + vector_rows[5 : 5 + extra].reshape(-1)
    hidden_act, gelu_back = jax.vjp(gelu_exact, hidden_pre)
    hidden_low = hidden_act.astype(jnp.bfloat16)
    feed_out = product(hidden_low, full_down) + vector_rows[5 + extra]
    result, norm_two_back = jax.vjp(
        post_norm, first_norm + feed_out, vector_rows[8 + extra], vector_rows[9 + extra]
    )
    layer_out = (result * valid_column).astype(jnp.bfloat16)
    cotangent = out_cotangent[0].astype(jnp.float32) * valid_column
    sum_adjoint, gain_two, shift_two = norm_two_back(cotangent)
    feed_low = sum_adjoint.astype(jnp.bfloat16)
    down_change = product_left(hidden_low, feed_low)
    bias_two = column_sums(feed_low)
    hidden_adjoint = product_back(feed_low, full_down)
    (pre_adjoint,) = gelu_back(hidden_adjoint)
    pre_low = pre_adjoint.astype(jnp.bfloat16)
    up_change = product_left(first_low, pre_low)
    bias_one = column_sums(pre_low)
    norm_adjoint = sum_adjoint + product_back(pre_low, full_up)
    mixture_adjoint, gain_one, shift_one = norm_one_back(norm_adjoint)
    branch_low = mixture_adjoint.astype(jnp.bfloat16)
    out_change = product_left(attended, branch_low)
    bias_out = column_sums(branch_low)
    attended_adjoint = product_back(branch_low, full_out).astype(jnp.bfloat16)
    spot_heads = split_heads(jnp.take(attended_adjoint, spots, axis=0))
    prob_adjoint = jnp.einsum(
        "ghd,jhd->hgj", spot_heads, split_heads(values_global), preferred_element_type=jnp.float32
    )
    score_adjoint = global_probs * (
        prob_adjoint - jnp.sum(global_probs * prob_adjoint, axis=-1, keepdims=True)
    )
    score_low = score_adjoint.astype(jnp.bfloat16)
    query_global_low = (
        (
            jnp.einsum(
                "hgj,jhd->ghd",
                score_low,
                split_heads(keys_global),
                preferred_element_type=jnp.float32,
            )
            * scale
        )
        .reshape(NG, D)
        .astype(jnp.bfloat16)
    )
    keys_global_low = (
        (
            jnp.einsum(
                "hgj,ghd->jhd",
                score_low,
                split_heads(query_global),
                preferred_element_type=jnp.float32,
            )
            * scale
        )
        .reshape(span, D)
        .astype(jnp.bfloat16)
    )
    values_global_low = (
        jnp.einsum("hgj,ghd->jhd", global_low, spot_heads, preferred_element_type=jnp.float32)
        .reshape(span, D)
        .astype(jnp.bfloat16)
    )
    local_adjoint = jnp.where(
        global_row[:, None], jnp.zeros_like(attended_adjoint), attended_adjoint
    )
    local_heads = split_heads(local_adjoint)
    query_pieces = []
    keys_total = jnp.zeros((span + 2 * half, H, HD), jnp.float32)
    values_total = jnp.zeros((span + 2 * half, H, HD), jnp.float32)
    keys_spot_total = jnp.zeros((NG, H, HD), jnp.float32)
    values_spot_total = jnp.zeros((NG, H, HD), jnp.float32)
    for index_block in range(span // block_rows):
        start = index_block * block_rows
        masked, raw_spot, allowed = block_scores(start)
        log_sum = log_sums[index_block]
        weights_local = jnp.where(allowed, jnp.exp(masked - log_sum), 0.0)
        weights_spot = jnp.exp(raw_spot - log_sum)
        adjoint_block = local_heads[start : start + block_rows]
        query_block = query_heads[start : start + block_rows]
        keys_slab = split_heads(keys_padded[start : start + slab_rows])
        values_slab = split_heads(values_padded[start : start + slab_rows])
        local_prob = jnp.einsum(
            "ihd,jhd->hij", adjoint_block, values_slab, preferred_element_type=jnp.float32
        )
        spot_prob = jnp.einsum(
            "ihd,jhd->hij", adjoint_block, values_spot, preferred_element_type=jnp.float32
        )
        center = jnp.sum(weights_local * local_prob, axis=-1, keepdims=True) + jnp.sum(
            weights_spot * spot_prob, axis=-1, keepdims=True
        )
        local_score = (weights_local * (local_prob - center)).astype(jnp.bfloat16)
        spot_score = (weights_spot * (spot_prob - center)).astype(jnp.bfloat16)
        query_part = jnp.einsum(
            "hij,jhd->ihd", local_score, keys_slab, preferred_element_type=jnp.float32
        )
        query_part = query_part + jnp.einsum(
            "hij,jhd->ihd", spot_score, keys_spot, preferred_element_type=jnp.float32
        )
        query_pieces.append((query_part * scale).reshape(block_rows, D).astype(jnp.bfloat16))
        keys_total = keys_total.at[start : start + slab_rows].add(
            jnp.einsum("hij,ihd->jhd", local_score, query_block, preferred_element_type=jnp.float32)
            * scale
        )
        keys_spot_total = (
            keys_spot_total
            + jnp.einsum(
                "hij,ihd->jhd", spot_score, query_block, preferred_element_type=jnp.float32
            )
            * scale
        )
        values_total = values_total.at[start : start + slab_rows].add(
            jnp.einsum(
                "hij,ihd->jhd",
                weights_local.astype(jnp.bfloat16),
                adjoint_block,
                preferred_element_type=jnp.float32,
            )
        )
        values_spot_total = values_spot_total + jnp.einsum(
            "hij,ihd->jhd",
            weights_spot.astype(jnp.bfloat16),
            adjoint_block,
            preferred_element_type=jnp.float32,
        )
    query_low = jnp.concatenate(query_pieces, axis=0)
    keys_low = (
        keys_total[half : half + span]
        .reshape(span, D)
        .at[spots]
        .add(keys_spot_total.reshape(NG, D))
        .astype(jnp.bfloat16)
    )
    values_low = (
        values_total[half : half + span]
        .reshape(span, D)
        .at[spots]
        .add(values_spot_total.reshape(NG, D))
        .astype(jnp.bfloat16)
    )
    in_change = jnp.stack(
        [
            product_left(sequence, query_low),
            product_left(sequence, keys_low),
            product_left(sequence, values_low),
            product_left(rows_global, query_global_low),
            product_left(sequence, keys_global_low),
            product_left(sequence, values_global_low),
        ]
    )
    token_adjoint = (
        mixture_adjoint
        + product_back(query_low, full_in[0])
        + product_back(keys_low, full_in[1])
        + product_back(values_low, full_in[2])
    )
    token_adjoint = (
        token_adjoint
        + product_back(keys_global_low, full_in[4])
        + product_back(values_global_low, full_in[5])
    )
    token_adjoint = token_adjoint.at[spots].add(product_back(query_global_low, full_in[3]))
    token_low = token_adjoint.astype(jnp.bfloat16)
    vector_change = jnp.concatenate(
        [
            jnp.stack(
                [
                    column_sums(query_low),
                    column_sums(values_low),
                    bias_out,
                    column_sums(query_global_low),
                    column_sums(values_global_low),
                ]
            ),
            bias_one.reshape(extra, D),
            jnp.stack([bias_two, gain_one, shift_one, gain_two, shift_two]),
        ],
        axis=0,
    )
    back_rows = lax.all_to_all(
        token_low[None], ("grp", "dp"), split_axis=1, concat_axis=0, tiled=True
    )
    back_rows = jnp.take(back_rows, deal, axis=0)
    token_gradient = lax.all_to_all(
        back_rows, ("grp", "dp"), split_axis=0, concat_axis=1, tiled=True
    )
    part_in, part_out, part_up, part_down = (
        lax.psum_scatter(
            in_change.astype(jnp.bfloat16), "grp", scatter_dimension=1, tiled=True
        ).astype(jnp.float32),
        lax.psum_scatter(
            out_change.astype(jnp.bfloat16), "grp", scatter_dimension=0, tiled=True
        ).astype(jnp.float32),
        lax.psum_scatter(
            up_change.astype(jnp.bfloat16), "grp", scatter_dimension=0, tiled=True
        ).astype(jnp.float32),
        lax.psum_scatter(
            down_change.astype(jnp.bfloat16), "grp", scatter_dimension=0, tiled=True
        ).astype(jnp.float32),
    )
    part_in, part_out, part_up, part_down, part_vectors = (
        lax.psum_scatter(
            part_in.astype(jnp.bfloat16), "dp", scatter_dimension=2, tiled=True
        ).astype(jnp.float32),
        lax.psum_scatter(
            part_out.astype(jnp.bfloat16), "dp", scatter_dimension=1, tiled=True
        ).astype(jnp.float32),
        lax.psum_scatter(
            part_up.astype(jnp.bfloat16), "dp", scatter_dimension=1, tiled=True
        ).astype(jnp.float32),
        lax.psum_scatter(
            part_down.astype(jnp.bfloat16), "dp", scatter_dimension=1, tiled=True
        ).astype(jnp.float32),
        lax.psum_scatter(
            vector_change.astype(jnp.bfloat16), "dp", scatter_dimension=1, tiled=True
        ).astype(jnp.float32),
    )
    part_vectors = lax.psum(part_vectors, "grp")
    step_count = jnp.float32(STEP)
    fix_first = 1.0 - jnp.power(jnp.float32(BETA_FIRST), step_count)
    fix_second = 1.0 - jnp.power(jnp.float32(BETA_SECOND), step_count)
    update_in, moment_in, square_in = adam_update(
        in_weights, part_in, first_in, second_in, WEIGHT_DECAY, fix_first, fix_second
    )
    update_out, moment_out, square_out = adam_update(
        out_weight, part_out, first_out, second_out, WEIGHT_DECAY, fix_first, fix_second
    )
    update_up, moment_up, square_up = adam_update(
        up_weight, part_up, first_up, second_up, WEIGHT_DECAY, fix_first, fix_second
    )
    update_down, moment_down, square_down = adam_update(
        down_weight, part_down, first_down, second_down, WEIGHT_DECAY, fix_first, fix_second
    )
    update_vectors, moment_vectors, square_vectors = adam_update(
        vectors, part_vectors, first_vectors, second_vectors, 0.0, fix_first, fix_second
    )
    return (
        layer_out[None],
        token_gradient,
        update_in,
        update_out,
        update_up,
        update_down,
        update_vectors,
        moment_in,
        moment_out,
        moment_up,
        moment_down,
        moment_vectors,
        square_in,
        square_out,
        square_up,
        square_down,
        square_vectors,
    )


def solution(mesh):
    return jax.shard_map(
        per_device,
        mesh=mesh,
        in_specs=(
            P(("grp", "dp"), None, None),
            P(("grp", "dp"), None, None),
            P(),
            P(),
            P(),
            P(None, "grp", "dp"),
            P("grp", "dp"),
            P("grp", "dp"),
            P("grp", "dp"),
            P(None, "dp"),
            P(None, "grp", "dp"),
            P("grp", "dp"),
            P("grp", "dp"),
            P("grp", "dp"),
            P(None, "dp"),
            P(None, "grp", "dp"),
            P("grp", "dp"),
            P("grp", "dp"),
            P("grp", "dp"),
            P(None, "dp"),
        ),
        out_specs=(
            P(("grp", "dp"), None, None),
            P(("grp", "dp"), None, None),
            P(None, "grp", "dp"),
            P("grp", "dp"),
            P("grp", "dp"),
            P("grp", "dp"),
            P(None, "dp"),
            P(None, "grp", "dp"),
            P("grp", "dp"),
            P("grp", "dp"),
            P("grp", "dp"),
            P(None, "dp"),
            P(None, "grp", "dp"),
            P("grp", "dp"),
            P("grp", "dp"),
            P("grp", "dp"),
            P(None, "dp"),
        ),
        check_vma=False,
    )
```

profile of v0, /device:TPU:0, one launch (start us, length us, event | category | flops | bytes accessed | tf_op | source)
XLA Modules:
  0.0 1176.5 jit_solution(1831720627038888687)
XLA Ops:
  13.1 37.5 %all-gather.8.cloned.1.call-done = bf16[6,128,1024]{2,1,0:T(8,128)(2,1)} async-done(((bf16[6,128,256]{2,1,0:T(8,128)(2,1)}), bf16[6,128,1024]{2,1,0:T(8,128)(2,1)}) %all-gather.8.cloned.1.call-update) | async-done | bytes 1572880 | tf_op jit(solution)/shard_map/all_gather | solution.py:105
  50.7 15.6 %all_gather.30 = bf16[128,1024]{1,0:T(8,128)(2,1)} all-gather(bf16[128,256]{1,0:T(8,128)(2,1)S(1)} %convert_element_type.249), channel_id=1, replica_groups=mesh['grp'=8,'dp'=4] {'dp'}, dimensions={1}, use_global_device_ids=true | all-gather | bytes 327680 | tf_op jit(solution)/shard_map/all_gather | solution.py:106
  66.4 13.3 %all-gather.14.cloned.1.call-done = bf16[128,4096]{1,0:T(8,128)(2,1)} async-done(((bf16[128,1024]{1,0:T(8,128)(2,1)}), bf16[128,4096]{1,0:T(8,128)(2,1)}) %all-gather.14.cloned.1.call-update) | async-done | bytes 1048592 | tf_op jit(solution)/shard_map/all_gather | solution.py:107
  85.5 12.8 %reduce.29 = bf16[1024,1024]{1,0:T(8,128)(2,1)S(1)} reduce(bf16[1024,1,1024]{2,1,0:T(2,128)(2,1)} %bitcast.247, bf16[]{:T(256)} %broadcast.451), dimensions={1}, to_apply=%bitcast.233.reduce_sub_computation | reduce | bytes 4194306
  108.1 46.1 %all-to-all-done = bf16[32,2,16384]{2,1,0:T(2,128)(2,1)S(1)} async-done(((bf16[32,2,16384]{2,1,0:T(2,128)(2,1)}), bf16[32,2,16384]{2,1,0:T(2,128)(2,1)S(1)}, u32[]{:S(2)}, u32[]{:S(2)}) %all-to-all-start) | async-done | bytes 2097184 | tf_op jit(solution)/shard_map/all_to_all | solution.py:94
  175.4 52.3 %all_gather.29 = bf16[14,1024]{1,0:T(8,128)(2,1)S(1)} all-gather(bf16[14,256]{1,0:T(8,128)(2,1)S(1)} %convert_element_type.235), channel_id=1, replica_groups=mesh['grp'=8,'dp'=4] {'dp'}, dimensions={1}, use_global_device_ids=true | all-gather | bytes 35840 | tf_op jit(solution)/shard_map/all_gather | solution.py:109
  311.4 15.6 %fusion.2 = (f32[16,512]{1,0:T(8,128)S(1)}, f32[16,512,1024]{2,1,0:T(8,128)}) fusion(pred[512,1024]{1,0:T(8,128)(4,1)} %get-tuple-element.255, bf16[512,16,64]{0,2,1:T(8,128)(2,1)S(1)} %bitcast.236, bf16[1024,16,64]{0,2,1:T(8,128)(2,1)} %bitcast.245), kind=kOutput, calls=%fused_computation.22 | convolution fusion | flops 1098899456 | bytes 37257216 | tf_op jit(solution)/shard_map/ihd,jhd->hij/dot_general | solution.py:146
  327.5 16.1 %select_reduce_fusion = f32[16,512]{1,0:T(8,128)S(1)} fusion(f32[16,512,1024]{2,1,0:T(8,128)} %get-tuple-element.215, f32[16,512]{1,0:T(8,128)S(1)} %max.23, pred[512,1024]{1,0:T(8,128)(4,1)S(1)} %copy-done.20), kind=kLoop, calls=%fused_computation.16 | loop fusion | flops 41934848 | bytes 34144256 | tf_op jit(solution)/shard_map/reduce_sum | solution.py:166
  345.5 17.5 %convolution_add_fusion = f32[16,64,512]{2,1,0:T(8,128)} fusion(f32[16,64,512]{2,1,0:T(8,128)} %fusion.56, bf16[1024,16,64]{0,2,1:T(8,128)(2,1)} %bitcast.282, f32[16,512]{1,0:T(8,128)S(1)} %log_add_fusion, f32[16,512,1024]{2,1,0:T(8,128)} %get-tuple-element.215, pred[512,1024]{1,0:T(8,128)(4,1)S(1)} %copy-done.21), kind=kOutput, calls=%fused_computation.137 | convolution fusion | flops 1116209152 | bytes 40402944 | tf_op jit(solution)/shard_map/hij,jhd->ihd/dot_general | solution.py:174
  366.0 15.6 %fusion.1 = (f32[16,512]{1,0:T(8,128)S(1)}, f32[16,512,1024]{2,1,0:T(8,128)}) fusion(pred[512,1024]{1,0:T(8,128)(4,1)} %get-tuple-element.254, bf16[512,16,64]{0,2,1:T(8,128)(2,1)S(1)} %bitcast.240, bf16[1024,16,64]{0,2,1:T(8,128)(2,1)} %bitcast.243), kind=kOutput, calls=%fused_computation.21 | convolution fusion | flops 1098899456 | bytes 37257216 | tf_op jit(solution)/shard_map/ihd,jhd->hij/dot_general | solution.py:146
  382.0 15.6 %select_reduce_fusion.1 = f32[16,512]{1,0:T(8,128)S(1)} fusion(f32[16,512,1024]{2,1,0:T(8,128)} %get-tuple-element.219, f32[16,512]{1,0:T(8,128)S(1)} %max.22, pred[512,1024]{1,0:T(8,128)(4,1)S(1)} %copy-done.24), kind=kLoop, calls=%fused_computation.19 | loop fusion | flops 41934848 | bytes 34144256 | tf_op jit(solution)/shard_map/reduce_sum | solution.py:166
  399.6 16.9 %convolution_add_fusion.1 = f32[16,64,512]{2,1,0:T(8,128)} fusion(f32[16,64,512]{2,1,0:T(8,128)} %fusion.58, bf16[1024,16,64]{0,2,1:T(8,128)(2,1)} %bitcast.280, f32[16,512]{1,0:T(8,128)S(1)} %log_add_fusion.1, f32[16,512,1024]{2,1,0:T(8,128)} %get-tuple-element.219, pred[512,1024]{1,0:T(8,128)(4,1)S(1)} %copy-done.25), kind=kOutput, calls=%fused_computation.138 | convolution fusion | flops 1116209152 | bytes 40402944 | tf_op jit(solution)/shard_map/hij,jhd->ihd/dot_general | solution.py:174
  437.2 48.2 %multiply_convert_fusion.2 = (bf16[1024,4096]{1,0:T(8,128)(2,1)}, f32[1024,4096]{1,0:T(8,128)}, f32[1024,4096]{1,0:T(8,128)}) fusion(f32[4096]{0:T(1024)S(1)} %bitcast.316, bf16[1024,4096]{1,0:T(8,128)(2,1)} %all-gather.16.cloned.1.call-done, bf16[1024,1024]{0,1:T(8,128)(2,1)S(1)} %fusion.95.clone.4), kind=kOutput, calls=%fused_computation.26 | convolution fusion | flops 8866758656 | bytes 52445184 | tf_op jit(solution)/shard_map/dot_general | solution.py:38
  485.4 14.9 %fusion.117 = (f32[1024]{0:T(1024)S(1)}, f32[1024,1024]{0,1:T(8,128)S(1)}) fusion(f32[1024]{0:T(1024)S(1)} %bitcast.318, bf16[1024,4096]{1,0:T(8,128)(2,1)} %get-tuple-element.185, bf16[4096,1024]{1,0:T(8,128)(2,1)} %all-gather.20.cloned.1.call-done, f32[1024]{0:T(1024)S(1)} %bitcast.313, f32[1024]{0:T(1024)S(1)} %bitcast.308, f32[1024]{0:T(1024)S(1)} %fusion.72, ...), kind=kOutput, calls=%fused_computation.257 | convolution fusion | flops 8597273600 | bytes 25190400 | tf_op jit(solution)/shard_map/dot_general | solution.py:38
  513.1 24.3 %fusion.99 = (bf16[4096]{0:T(1024)(128)(2,1)}, bf16[1024,4096]{1,0:T(8,128)(2,1)}) fusion(f32[1024,4096]{1,0:T(8,128)} %get-tuple-element.186, f32[1024,4096]{1,0:T(8,128)} %get-tuple-element.226, f32[4096]{0:T(1024)S(1)} %bitcast.317, bf16[1024,1024]{0,1:T(8,128)(2,1)} %get-tuple-element.166, bf16[4096,1024]{1,0:T(8,128)(2,1)} %all-gather.20.cloned.1.call-done), kind=kOutput, calls=%fused_computation.249 | convolution fusion | flops 8657039360 | bytes 52453376 | tf_op jit(solution)/shard_map/dot_general | solution.py:42
  537.5 17.5 %multiply_reduce_fusion.2 = (bf16[1024]{0:T(1024)(128)(2,1)}, f32[1024]{0:T(1024)S(1)}, bf16[1024]{0:T(1024)(128)(2,1)}, f32[1024,1024]{0,1:T(8,128)S(1)}) fusion(f32[1024,1024]{0,1:T(8,128)S(1)} %copy-done.10, f32[1024]{0:T(1024)S(1)} %fusion.72, f32[1024]{0:T(1024)S(1)} %broadcast_multiply_fusion.1, f32[1024]{0:T(1024)S(1)} %bitcast.309, ...), kind=kOutput, calls=%fused_computation.59 | convolution fusion | flops 8608805888 | bytes 31502336 | tf_op jit(solution)/shard_map/dot_general | solution.py:42
  570.0 17.8 %convolution_bitcast_fusion = f32[1024,16,64]{0,2,1:T(8,128)} fusion(bf16[512,16,64]{0,2,1:T(8,128)(2,1)S(1)} %bitcast.265, f32[16,512]{1,0:T(8,128)S(1)} %copy-done.61, f32[16,512,1024]{2,1,0:T(8,128)} %get-tuple-element.219, pred[512,1024]{1,0:T(8,128)(4,1)S(1)} %copy-done.26), kind=kOutput, calls=%fused_computation.86 | convolution fusion | flops 1115684864 | bytes 39354368 | tf_op jit(solution)/shard_map/hij,ihd->jhd/dot_general | solution.py:317
  587.8 15.1 %convolution_convert_fusion = bf16[4096,1024]{1,0:T(8,128)(2,1)} fusion(bf16[1024,4096]{1,0:T(8,128)(2,1)} %get-tuple-element.185, bf16[1024,1024]{0,1:T(8,128)(2,1)} %get-tuple-element.166), kind=kOutput, calls=%fused_computation.42 | convolution fusion | flops 8594128896 | bytes 18874368 | tf_op jit(solution)/shard_map/dot_general | solution.py:48
  602.9 26.9 %multiply_reduce_fusion = (f32[16,512]{1,0:T(8,128)S(1)}, f32[16,512,1024]{2,1,0:T(8,128)}) fusion(f32[16,512]{1,0:T(8,128)S(1)} %copy-done.59, f32[16,512,1024]{2,1,0:T(8,128)} %get-tuple-element.215, pred[512,1024]{1,0:T(8,128)(4,1)S(1)} %copy-done.22, bf16[512,16,64]{0,2,1:T(8,128)(2,1)S(1)} %bitcast.269, bf16[1024,16,64]{0,2,1:T(8,128)(2,1)} %bitcast.283), kind=kOutput, calls=%fused_computation.12 | convolution fusion | flops 1124065280 | bytes 70844416 | tf_op jit(solution)/shard_map/ihd,jhd->hij/dot_general | solution.py:287
  635.5 22.9 %fusion.18 = f32[1536,16,64]{0,2,1:T(8,128)} fusion(f32[1536,16,64]{0,2,1:T(8,128)} %scatter-add.44, bf16[512,16,64]{0,2,1:T(8,128)(2,1)} %bitcast.270, f32[16,512]{1,0:T(8,128)S(1)} %copy-done.59, f32[16,512,1024]{2,1,0:T(8,128)} %get-tuple-element.215, pred[512,1024]{1,0:T(8,128)(4,1)S(1)} %copy-done.22), kind=kOutput, calls=%fused_computation.56 | convolution fusion | flops 1116733440 | bytes 43548672 | tf_op jit(solution)/shard_map/hij,ihd->jhd/dot_general | solution.py:317
  686.1 27.2 %multiply_reduce_fusion.1 = (f32[16,512]{1,0:T(8,128)S(1)}, f32[16,512,1024]{2,1,0:T(8,128)}) fusion(f32[16,512]{1,0:T(8,128)S(1)} %copy-done.61, f32[16,512,1024]{2,1,0:T(8,128)} %get-tuple-element.219, pred[512,1024]{1,0:T(8,128)(4,1)S(1)} %copy-done.26, bf16[512,16,64]{0,2,1:T(8,128)(2,1)S(1)} %bitcast.268, bf16[1024,16,64]{0,2,1:T(8,128)(2,1)S(1)} %bitcast.281), kind=kOutput, calls=%fused_computation.14 | convolution fusion | flops 1124065280 | bytes 70844416 | tf_op jit(solution)/shard_map/ihd,jhd->hij/dot_general | solution.py:287
  719.7 27.6 %multiply_convert_fusion.1 = bf16[16,512,1024]{2,1,0:T(8,128)(2,1)} fusion(f32[16,512,1024]{2,1,0:T(8,128)} %get-tuple-element.235, f32[16,512]{1,0:T(8,128)S(1)} %add.461, f32[16,512]{1,0:T(8,128)S(1)} %copy-done.61, f32[16,512,1024]{2,1,0:T(8,128)} %get-tuple-element.219, pred[512,1024]{1,0:T(8,128)(4,1)S(1)} %copy-done.27), kind=kLoop, calls=%fused_computation.13 | loop fusion | flops 58720256 | bytes 84475904 | tf_op jit(solution)/shard_map/convert_element_type | solution.py:296
  759.6 14.9 %convolution_convert_fusion.1 = bf16[1024,4096]{1,0:T(8,128)(2,1)} fusion(bf16[1024,4096]{1,0:T(8,128)(2,1)} %get-tuple-element.168, f32[1024,1024]{0,1:T(8,128)S(1)} %copy-done.11, f32[1024]{0:T(1024)S(1)} %bitcast.314, f32[1024]{0:T(1024)S(1)} %bitcast.311, f32[1024]{0:T(1024)S(1)} %copy-done.80, f32[1024]{0:T(1024)S(1)} %copy-done.76), kind=kOutput, calls=%fused_computation.43 | convolution fusion | flops 8599371776 | bytes 20987904 | tf_op jit(solution)/shard_map/dot_general | solution.py:48
  775.6 31.9 %multiply_convert_fusion = bf16[16,512,1024]{2,1,0:T(8,128)(2,1)} fusion(f32[16,512,1024]{2,1,0:T(8,128)} %get-tuple-element.239, f32[16,512]{1,0:T(8,128)S(1)} %add.463, f32[16,512]{1,0:T(8,128)S(1)} %copy-done.59, f32[16,512,1024]{2,1,0:T(8,128)} %get-tuple-element.215, pred[512,1024]{1,0:T(8,128)(4,1)S(1)} %copy-done.23), kind=kLoop, calls=%fused_computation.11 | loop fusion | flops 58720256 | bytes 84475904 | tf_op jit(solution)/shard_map/convert_element_type | solution.py:296
  807.5 12.6 %fusion.19 = f32[1536,16,64]{0,2,1:T(8,128)} fusion(f32[1536,16,64]{0,2,1:T(8,128)} %scatter-add.34, bf16[512,16,64]{0,2,1:T(8,128)(2,1)S(1)} %bitcast.238, bf16[16,512,1024]{2,1,0:T(8,128)(2,1)} %multiply_convert_fusion), kind=kOutput, calls=%fused_computation.58 | convolution fusion | flops 1075838976 | bytes 26214400 | tf_op jit(solution)/shard_map/hij,ihd->jhd/dot_general | solution.py:306
  862.8 12.5 %bitcast_reduce_fusion.2 = (bf16[16,64]{1,0:T(8,128)(2,1)S(1)}, bf16[16,64,512]{2,1,0:T(8,128)(2,1)}) fusion(f32[16,64,512]{2,1,0:T(8,128)} %fusion.118, bf16[1024,16,64]{0,2,1:T(8,128)(2,1)S(1)} %bitcast.244, bf16[16,512,1024]{2,1,0:T(8,128)(2,1)} %multiply_convert_fusion.1), kind=kOutput, calls=%fused_computation.150 | convolution fusion | flops 1075837952 | bytes 22022144 | tf_op jit(solution)/shard_map/hij,jhd->ihd/dot_general | solution.py:298
  948.1 12.8 %reduce.30 = bf16[1024,1024]{1,0:T(8,128)(2,1)S(1)} reduce(bf16[1024,1,1024]{2,1,0:T(2,128)(2,1)} %bitcast.248, bf16[]{:T(256)} %broadcast.451), dimensions={1}, to_apply=%bitcast.232.reduce_sub_computation | reduce | bytes 4194306
  977.3 38.7 %all-to-all-done.2 = bf16[32,2,16384]{2,1,0:T(2,128)(2,1)S(1)} async-done(((bf16[32,2,16384]{2,1,0:T(2,128)(2,1)}), bf16[32,2,16384]{2,1,0:T(2,128)(2,1)S(1)}, u32[]{:S(2)}, u32[]{:S(2)}) %all-to-all-start.2) | async-done | bytes 2097184 | tf_op jit(solution)/shard_map/all_to_all | solution.py:384
  1039.8 27.1 %psum.7 = f32[14,256]{1,0:T(8,128)} all-reduce(bf16[14,256]{1,0:T(8,128)(2,1)} %reduce-scatter.26.cloned.1.call-done), channel_id=1, replica_groups=mesh['grp'=8,'dp'=4] {'grp'}, use_global_device_ids=true, to_apply=%region_49.52 | all-reduce | flops 3584 | bytes 21504 | tf_op jit(solution)/shard_map/psum | solution.py:422
  1070.1 33.0 %all-to-all-done.3 = bf16[32,32,1024]{2,1,0:T(8,128)(2,1)S(1)} async-done(((bf16[32,32,1024]{2,1,0:T(8,128)(2,1)}), bf16[32,32,1024]{2,1,0:T(8,128)(2,1)S(1)}, u32[]{:S(2)}, u32[]{:S(2)}) %all-to-all-start.3) | async-done | bytes 2097184 | tf_op jit(solution)/shard_map/all_to_all | solution.py:388
  1105.8 23.3 %reduce-scatter.20.cloned.1.call-done = bf16[128,1024]{1,0:T(8,128)(2,1)} async-done(((bf16[128,4096]{1,0:T(8,128)(2,1)}), bf16[128,1024]{1,0:T(8,128)(2,1)}) %reduce-scatter.20.cloned.1.call-update) | async-done | bytes 262160 | tf_op jit(solution)/shard_map/reduce_scatter | solution.py:412
  1131.8 33.4 %reduce-scatter.12.cloned.1.call-done = bf16[6,128,256]{2,1,0:T(8,128)(2,1)} async-done(((bf16[6,128,1024]{2,1,0:T(8,128)(2,1)}), bf16[6,128,256]{2,1,0:T(8,128)(2,1)}) %reduce-scatter.12.cloned.1.call-update) | async-done | bytes 393232 | tf_op jit(solution)/shard_map/reduce_scatter | solution.py:406
  (446 shorter events, 401.1 us)
Async XLA Ops:
  7.2 72.5 %copy-start.52 = (bf16[1,1024,1024]{2,1,0:T(8,128)(2,1)S(1)}, bf16[1,1024,1024]{2,1,0:T(8,128)(2,1)}, u32[]{:S(2)}) copy-start(bf16[1,1024,1024]{2,1,0:T(8,128)(2,1)} %param.32) | copy-start | bytes 6291460
  7.2 43.4 %all-gather.8.cloned.1.call-start = ((), (), s32[]{:S(2)}) async-start(), calls=%async_computation.13 | async-start | bytes 1966080 | tf_op jit(solution)/shard_map/all_gather | solution.py:105
  9.4 70.3 %all-gather.14.cloned.1.call-start = ((), (), s32[]{:S(2)}) async-start(), calls=%async_computation.16 | async-start | bytes 1310720 | tf_op jit(solution)/shard_map/all_gather | solution.py:107
  11.2 230.0 %all-gather.18.cloned.1.call-start = ((), (), s32[]{:S(2)}) async-start(), calls=%async_computation.18 | async-start | bytes 1310720 | tf_op jit(solution)/shard_map/all_gather | solution.py:108
  13.1 231.8 %all-gather.10.cloned.1.call-start = ((), (), s32[]{:S(2)}) async-start(), calls=%async_computation.14 | async-start | bytes 14155776 | tf_op jit(solution)/shard_map/all_gather | solution.py:112
  50.6 378.2 %all-gather.12.cloned.1.call-start = ((), (), s32[]{:S(2)}) async-start(), calls=%async_computation.15 | async-start | bytes 2359296 | tf_op jit(solution)/shard_map/all_gather | solution.py:113
  66.3 370.9 %all-gather.16.cloned.1.call-start = ((), (), s32[]{:S(2)}) async-start(), calls=%async_computation.17 | async-start | bytes 9437184 | tf_op jit(solution)/shard_map/all_gather | solution.py:114
  101.1 53.2 %all-to-all-start = ((bf16[32,2,16384]{2,1,0:T(2,128)(2,1)}), bf16[32,2,16384]{2,1,0:T(2,128)(2,1)S(1)}, u32[]{:S(2)}, u32[]{:S(2)}) async-start(bf16[32,2,16384]{2,1,0:T(2,128)(2,1)} %reshape.643), calls=%async_computation | async-start | bytes 4194304 | tf_op jit(solution)/shard_map/all_to_all | solution.py:94
  169.2 63.7 %copy-start.111 = (s32[32]{0:T(128)S(1)}, s32[32]{0:T(128)}, u32[]{:S(2)}) copy-start(s32[32]{0:T(128)} %param.34) | copy-start | bytes 388
  169.2 72.2 %all-to-all-start.1 = ((bf16[32,32,1024]{2,1,0:T(8,128)(2,1)}), bf16[32,32,1024]{2,1,0:T(8,128)(2,1)S(1)}, u32[]{:S(2)}, u32[]{:S(2)}) async-start(bf16[32,32,1024]{2,1,0:T(8,128)(2,1)} %broadcast_select_fusion.1), calls=%async_computation.1 | async-start | bytes 4194304 | tf_op jit(solution)/shard_map/all_to_all | solution.py:96
  173.4 312.0 %all-gather.20.cloned.1.call-start = ((), (), s32[]{:S(2)}) async-start(), calls=%async_computation.19 | async-start | bytes 9437184 | tf_op jit(solution)/shard_map/all_gather | solution.py:115
  235.4 50.2 %copy-start.96 = (pred[64]{0:T(512)(128)(4,1)}, pred[64]{0:T(512)(128)(4,1)S(1)}, u32[]{:S(2)}) copy-start(pred[64]{0:T(512)(128)(4,1)S(1)} %get-tuple-element.187) | copy-start | bytes 196
  238.1 46.8 %copy-start.89 = (s32[1024]{0:T(1024)}, s32[1024]{0:T(1024)S(1)}, u32[]{:S(2)}) copy-start(s32[1024]{0:T(1024)S(1)} %pad_clamp_fusion.1) | copy-start | bytes 12292
  241.2 734.2 %reduce-scatter.14.cloned.1.call-start = ((), (), s32[]{:S(2)}) async-start(), calls=%async_computation.22 | async-start | bytes 2359296 | tf_op jit(solution)/shard_map/reduce_scatter | solution.py:395
  286.7 111.0 %copy-start.44 = (bf16[64,16,64]{2,1,0:T(8,128)(2,1)}, bf16[64,16,64]{2,1,0:T(8,128)(2,1)S(1)}, u32[]{:S(2)}) copy-start(bf16[64,16,64]{2,1,0:T(8,128)(2,1)S(1)} %reshape.521) | copy-start | bytes 393220
  288.7 109.1 %copy-start = (f32[16,512,64]{1,2,0:T(8,128)}, f32[16,512,64]{1,2,0:T(8,128)S(1)}, u32[]{:S(2)}) copy-start(f32[16,512,64]{1,2,0:T(8,128)S(1)} %get-tuple-element.221) | copy-start | bytes 6291460
  434.5 120.5 %copy-start.75 = (f32[1024]{0:T(1024)}, f32[1024]{0:T(1024)S(1)}, u32[]{:S(2)}) copy-start(f32[1024]{0:T(1024)S(1)} %broadcast_multiply_fusion.1) | copy-start | bytes 12292
  435.0 50.3 %copy-start.81 = (f32[1024]{0:T(1024)}, f32[1024]{0:T(1024)S(1)}, u32[]{:S(2)}) copy-start(f32[1024]{0:T(1024)S(1)} %multiply_reduce_fusion.6) | copy-start | bytes 12292
  435.1 120.0 %copy-start.79 = (f32[1024]{0:T(1024)}, f32[1024]{0:T(1024)S(1)}, u32[]{:S(2)}) copy-start(f32[1024]{0:T(1024)S(1)} %fusion.72) | copy-start | bytes 12292
  437.2 48.2 %copy-start.102 = (f32[1,1024]{1,0:T(1,128)S(1)}, f32[1,1024]{1,0:T(1,128)}, u32[]{:S(2)}) copy-start(f32[1,1024]{1,0:T(1,128)} %get-tuple-element.202) | copy-start | bytes 12292
  563.6 412.6 %reduce-scatter.22.cloned.1.call-start = ((), (), s32[]{:S(2)}) async-start(), calls=%async_computation.26 | async-start | bytes 9437184 | tf_op jit(solution)/shard_map/reduce_scatter | solution.py:401
  629.8 346.9 %reduce-scatter.18.cloned.1.call-start = ((), (), s32[]{:S(2)}) async-start(), calls=%async_computation.24 | async-start | bytes 9437184 | tf_op jit(solution)/shard_map/reduce_scatter | solution.py:398
  774.6 260.8 %reduce-scatter.10.cloned.1.call-start = ((), (), s32[]{:S(2)}) async-start(), calls=%async_computation.20 | async-start | bytes 14155776 | tf_op jit(solution)/shard_map/reduce_scatter | solution.py:392
  963.8 52.2 %all-to-all-start.2 = ((bf16[32,2,16384]{2,1,0:T(2,128)(2,1)}), bf16[32,2,16384]{2,1,0:T(2,128)(2,1)S(1)}, u32[]{:S(2)}, u32[]{:S(2)}) async-start(bf16[32,2,16384]{2,1,0:T(2,128)(2,1)} %reshape.645), calls=%async_computation.2 | async-start | bytes 4194304 | tf_op jit(solution)/shard_map/all_to_all | solution.py:384
  968.9 70.9 %reduce-scatter.26.cloned.1.call-start = ((), (), s32[]{:S(2)}) async-start(), calls=%async_computation.28 | async-start | bytes 40960 | tf_op jit(solution)/shard_map/reduce_scatter | solution.py:418
  975.3 93.0 %reduce-scatter.16.cloned.1.call-start = ((), (), s32[]{:S(2)}) async-start(), calls=%async_computation.23 | async-start | bytes 327680 | tf_op jit(solution)/shard_map/reduce_scatter | solution.py:409
  976.1 127.1 %reduce-scatter.24.cloned.1.call-start = ((), (), s32[]{:S(2)}) async-start(), calls=%async_computation.27 | async-start | bytes 1310720 | tf_op jit(solution)/shard_map/reduce_scatter | solution.py:415
  976.6 152.4 %reduce-scatter.20.cloned.1.call-start = ((), (), s32[]{:S(2)}) async-start(), calls=%async_computation.25 | async-start | bytes 1310720 | tf_op jit(solution)/shard_map/reduce_scatter | solution.py:412
  1030.9 72.2 %all-to-all-start.3 = ((bf16[32,32,1024]{2,1,0:T(8,128)(2,1)}), bf16[32,32,1024]{2,1,0:T(8,128)(2,1)S(1)}, u32[]{:S(2)}, u32[]{:S(2)}) async-start(bf16[32,32,1024]{2,1,0:T(8,128)(2,1)} %broadcast_select_fusion), calls=%async_computation.3 | async-start | bytes 4194304 | tf_op jit(solution)/shard_map/all_to_all | solution.py:388
  1035.3 67.9 %copy-start.55 = (f32[512,256]{1,0:T(8,128)S(1)}, f32[512,256]{1,0:T(8,128)}, u32[]{:S(2)}) copy-start(f32[512,256]{1,0:T(8,128)} %param.40) | copy-start | bytes 1572868
  1035.3 130.0 %reduce-scatter.12.cloned.1.call-start = ((), (), s32[]{:S(2)}) async-start(), calls=%async_computation.21 | async-start | bytes 1966080 | tf_op jit(solution)/shard_map/reduce_scatter | solution.py:406
  1039.8 125.4 %copy-start.51 = (f32[6,128,256]{2,1,0:T(8,128)S(1)}, f32[6,128,256]{2,1,0:T(8,128)}, u32[]{:S(2)}) copy-start(f32[6,128,256]{2,1,0:T(8,128)} %param.37) | copy-start | bytes 2359300
  (103 other events, 851.8 us)
Sparse Core Ops, SparseCore 0:
  10.2 40.3 all-gather.7
  52.8 26.8 all-gather.13
  81.8 34.3 all-gather.17
  117.9 97.0 all-gather.9
  216.8 27.5 all-gather.11
  246.2 54.3 all-gather.15
  302.5 54.3 all-gather.19
  563.7 41.2 reduce-scatter.13
  629.9 71.2 reduce-scatter.21
  774.7 72.0 reduce-scatter.17
  901.8 108.9 reduce-scatter.9
  1013.5 18.6 reduce-scatter.25
  1034.4 22.2 reduce-scatter.15
  1058.9 39.6 reduce-scatter.23
  1100.8 28.2 reduce-scatter.19
  1131.3 33.8 reduce-scatter.11
where the time goes:
time: 1190 us; the launch traced here: 1180 us
  matrix products  466 us (39%)
  waiting for transfers between devices  228 us (19%)
  other arithmetic  195 us (16%)
  local copies, waits for them, and re-layouts  157 us (13%)
  blocking collectives  95 us (8%)
  starting transfers between devices  18.8 us (2%)
  between operations  17.7 us (1%)
    dot_general x9, matrix products, product(): return jnp.dot(left_side, right_side, preferred_element_type=jnp.float32)  96.7 us
    dot_general x9, matrix products, product_back(): lax.dot_general(left_side, right_side, (((1,), (1,)), ((), ())), preferre...  74.2 us
    convert_element_type x2, other arithmetic, per_device(): local_score = (weights_local * (local_prob - center)).astype(jnp.bfloat16)  59.5 us
    dot_general x9, matrix products, product_left(): lax.dot_general(left_side, right_side, (((0,), (0,)), ((), ())), preferre...  57.1 us
    unnamed x243, local copies, waits for them, and re-layouts  54.9 us
    dot_general x2, matrix products, per_device(): jnp.einsum('ihd,jhd->hij', adjoint_block, values_slab, preferred_element_...  54.1 us
    all_gather x1, blocking collectives, per_device(): lax.all_gather(low_vectors, 'dp', axis=1, tiled=True)  52.3 us
    all_to_all x1, waiting for transfers between devices, per_device(): lax.all_to_all(tokens, ('grp', 'dp'), split_axis=1, concat_axis=0, tiled=...  46.1 us
  transfers between devices with their start and end apart: 20, of which 7 were waited for; matrix products, arithmetic and copies ran while one was open for 61% of the time, Pallas kernels for 0%

commit v1 on v0

v1 whole, which is shorter than its diff:
```python
import jax
import jax.numpy as jnp
import numpy as np
from jax import lax
from jax.experimental import pallas as pl
from jax.experimental.pallas import tpu as pltpu
from jax.sharding import PartitionSpec as P

D = 1024
H = 16
HD = 64
FF = 4096
W = 512
NG = 64
STEP = 10

EPS_NORM = 1e-05
WEIGHT_DECAY = 0.1
BETA_FIRST = 0.5
BETA_SECOND = 0.999
EPS_ADAM = 1e-08
NEGATIVE = -1e30

MESH = pl.DeviceIdType.MESH
MIB = 1 << 20
BF = jnp.bfloat16
F32 = jnp.float32
LANES = 128
ROWS = 256
ANYSPEC = pl.BlockSpec(memory_space=pl.ANY)
VMEMSPEC = pl.BlockSpec(memory_space=pltpu.VMEM)


def product(left_side, right_side):
    return jnp.dot(left_side, right_side, preferred_element_type=F32)


def product_back(left_side, right_side):
    return lax.dot_general(
        left_side, right_side, (((1,), (1,)), ((), ())), preferred_element_type=F32
    )


def product_left(left_side, right_side):
    return lax.dot_general(
        left_side, right_side, (((0,), (0,)), ((), ())), preferred_element_type=F32
    )


def column_sums(matrix):
    return jnp.sum(matrix.astype(F32), axis=0)


def adam_update(weight, gradient, moment, square, decay_rate, fix_first, fix_second):
    moment_new = BETA_FIRST * moment + (1.0 - BETA_FIRST) * gradient
    square_new = BETA_SECOND * square + (1.0 - BETA_SECOND) * gradient * gradient
    update = moment_new / fix_first / (jnp.sqrt(square_new / fix_second) + EPS_ADAM)
    return (update + decay_rate * weight, moment_new, square_new)


class Spot:
    def __init__(self, groups, depth):
        self.nb = groups // 4
        self.nz = depth
        self.groups = groups
        g = lax.axis_index("grp")
        self.g = g
        self.z = lax.axis_index("dp")
        self.c = lax.rem(g, 2)
        self.b = lax.rem(lax.div(g, 2), self.nb)
        self.a = lax.div(g, 2 * self.nb)

    def at(self, a=None, b=None, c=None, z=None):
        a = self.a if a is None else a
        b = self.b if b is None else b
        c = self.c if c is None else c
        z = self.z if z is None else z
        return ((a * self.nb + b) * 2 + c, z)

    def b_off(self, i):
        return lax.rem(self.b + i, self.nb)

    def z_off(self, i):
        return lax.rem(self.z + i, self.nz)

    def neighbours(self):
        out = [self.at(a=1 - self.a), self.at(c=1 - self.c)]
        out += [self.at(b=self.b_off(i)) for i in range(1, self.nb)]
        out += [self.at(z=self.z_off(i)) for i in range(1, self.nz)]
        return out


def greet(targets):
    barrier = pltpu.get_barrier_semaphore()
    for target in targets:
        pl.semaphore_signal(barrier, inc=1, device_id=target, device_id_type=MESH)
    pl.semaphore_wait(barrier, len(targets))


class Sems:
    def __init__(self, send, recv):
        self.send, self.recv, self.used = send, recv, 0

    def copy(self, src, dst, target):
        i = self.used
        self.used += 1
        return pltpu.make_async_remote_copy(
            src_ref=src,
            dst_ref=dst,
            send_sem=self.send.at[i],
            recv_sem=self.recv.at[i],
            device_id=target,
            device_id_type=MESH,
        )


def start_all(copies):
    for copy in copies:
        copy.start()


def recv_all(copies):
    for copy in copies:
        copy.wait_recv()


def send_done(copies):
    for copy in copies:
        copy.wait_send()


def gather_copies(nb, nz):
    return (nz - 1) + 1 + (nb - 1) + (nb - 1) + 1 + 1


class GatherPiece:
    def __init__(self, spot, sems, local_sem, src, out):
        a, b, c, z = spot.a, spot.b, spot.c, spot.z
        rows, width = src.shape
        half = rows // 2
        own = pl.ds(pl.multiple_of(z * width, LANES), width)
        top, low = pl.ds(0, half), pl.ds(half, half)
        shard = src
        mine = out.at[a, b, c, :, own]
        self.local = pltpu.make_async_copy(shard, mine, local_sem)
        self.phases = [
            [sems.copy(shard, mine, spot.at(z=spot.z_off(i))) for i in range(1, spot.nz)],
            [sems.copy(out.at[a, b, c, top], out.at[a, b, c, top], spot.at(a=1 - a))]
            + [
                sems.copy(out.at[a, b, c, low], out.at[a, b, c, low], spot.at(b=spot.b_off(i)))
                for i in range(1, spot.nb)
            ],
            [
                sems.copy(out.at[:, b, c, top], out.at[:, b, c, top], spot.at(b=spot.b_off(i)))
                for i in range(1, spot.nb)
            ]
            + [sems.copy(out.at[a, :, c, low], out.at[a, :, c, low], spot.at(a=1 - a))],
            [sems.copy(out.at[:, :, c], out.at[:, :, c], spot.at(c=1 - c))],
        ]

    def start(self, p):
        if p == 0:
            self.local.start()
        if p == 1:
            self.local.wait()
        start_all(self.phases[p])

    def arrive(self, p):
        recv_all(self.phases[p])

    def close(self):
        for phase in self.phases:
            send_done(phase)


class Swap:
    def __init__(self, spot, sems, local_sem, src, dst):
        devices = spot.groups * spot.nz
        me = spot.g * spot.nz + spot.z
        self.local = pltpu.make_async_copy(src.at[me], dst.at[me], local_sem)
        self.copies = []
        for i in range(1, devices):
            other = lax.rem(me + i, devices)
            self.copies.append(
                sems.copy(src.at[other], dst.at[me], (lax.div(other, spot.nz), lax.rem(other, spot.nz)))
            )

    def start(self, part, parts):
        if part == 0:
            self.local.start()
        n = len(self.copies)
        start_all(self.copies[part * n // parts : (part + 1) * n // parts])

    def finish(self):
        self.local.wait()
        recv_all(self.copies)
        send_done(self.copies)


def timeline(pieces, times, which=(0, 1, 2, 3, 4)):
    phases = len(pieces[0].phases)
    steps = {}
    for t in reversed(range(len(pieces))):
        for p in which:
            steps.setdefault(times[t][p], []).append((t, p))

    def run(events):
        for t, p in events:
            if p > 0:
                pieces[t].arrive(p - 1)
            if p < phases:
                pieces[t].start(p)
            else:
                pieces[t].close()

    return {s: (lambda events=events: run(events)) for s, events in steps.items()}


class Ticks:
    def __init__(self, per):
        self.per, self.actions = per, {}

    def add(self, tick, action):
        self.actions.setdefault(tick, []).append(action)

    def add_all(self, actions):
        for tick, action in actions.items():
            self.add(tick, action)

    def here(self, c, first, last):
        for tick in sorted(self.actions):
            if tick % self.per == c and first <= tick // self.per <= last:

                @pl.when(pl.program_id(0) == tick // self.per)
                def _(mine=self.actions[tick]):
                    for action in mine:
                        action()


def during(first, last):
    return pl.when(jnp.logical_and(pl.program_id(0) >= first, pl.program_id(0) <= last))


def in_chunks(span, body):
    def step(i, carry):
        body(pl.ds(pl.multiple_of(i * ROWS, ROWS), ROWS))
        return carry

    lax.fori_loop(0, span // ROWS, step, 0)


def slot_times(slot, count):
    return [
        [0 if t == 0 else slot(t - 1) + 1, slot(t), slot(t + 1) + 1, slot(t + 2) + 2, slot(t + 3) + 3]
        for t in range(count)
    ]


def reduce_copies(nb, nz):
    return 1 + (nb - 1) + 1 + 1 + (nb - 1) + (nz - 1)


class ReducePiece:
    def __init__(self, spot, sems, local_sem, src, width, boxes, finish):
        self.spot, self.finish, self.width = spot, finish, width
        tile, self.r0, self.r1b, self.r1a, self.r2a, self.r2b, self.r3 = boxes
        a, b, c, z = spot.a, spot.b, spot.c, spot.z
        self.acc = acc = tile.at[:, :, c] if src is None else tile.at[:, :, 0]
        other = (tile if src is None else src).at[:, :, 1 - c]
        half = tile.shape[-2] // 2
        self.half = half
        top, low = pl.ds(0, half), pl.ds(half, half)
        self.local = None if src is None else pltpu.make_async_copy(src.at[:, :, c], acc, local_sem)
        columns = lambda zz: pl.ds(pl.multiple_of(zz * self.width, LANES), self.width)
        self.own_columns = columns(z)
        self.phases = [
            [sems.copy(other, self.r0, spot.at(c=1 - c))],
            [
                sems.copy(acc.at[:, spot.b_off(i), top], self.r1b.at[i - 1], spot.at(b=spot.b_off(i)))
                for i in range(1, spot.nb)
            ]
            + [sems.copy(acc.at[1 - a, :, low], self.r1a, spot.at(a=1 - a))],
            [sems.copy(acc.at[1 - a, b, top], self.r2a, spot.at(a=1 - a))]
            + [
                sems.copy(acc.at[a, spot.b_off(i), low], self.r2b.at[i - 1], spot.at(b=spot.b_off(i)))
                for i in range(1, spot.nb)
            ],
            [
                sems.copy(
                    acc.at[a, b, :, columns(spot.z_off(i))], self.r3.at[i - 1], spot.at(z=spot.z_off(i))
                )
                for i in range(1, spot.nz)
            ],
        ]

    def start(self, p):
        if p == 0 and self.local is not None:
            self.local.start()
        start_all(self.phases[p])

    def arrive(self, p):
        spot, acc = self.spot, self.acc
        a, b = spot.a, spot.b
        top, low = pl.ds(0, self.half), pl.ds(self.half, self.half)
        recv_all(self.phases[p])
        if p == 0:
            if self.local is not None:
                self.local.wait()
            for i in range(2):
                for j in range(spot.nb):
                    acc[i, j] = (acc[i, j].astype(F32) + self.r0[i, j].astype(F32)).astype(BF)
        if p == 1:
            for i in range(2):
                total = acc[i, b, top].astype(F32)
                for k in range(spot.nb - 1):
                    total = total + self.r1b[k, i].astype(F32)
                acc[i, b, top] = total.astype(BF)
            for j in range(spot.nb):
                acc[a, j, low] = (acc[a, j, low].astype(F32) + self.r1a[j].astype(F32)).astype(BF)
        if p == 2:
            acc[a, b, top] = (acc[a, b, top].astype(F32) + self.r2a[...].astype(F32)).astype(BF)
            total = acc[a, b, low].astype(F32)
            for k in range(spot.nb - 1):
                total = total + self.r2b[k].astype(F32)
            acc[a, b, low] = total.astype(BF)
        if p == 3:
            total = acc[a, b, :, self.own_columns].astype(F32)
            for k in range(spot.nz - 1):
                total = total + self.r3[k].astype(F32)
            self.finish(total)

    def close(self):
        for phase in self.phases:
            send_done(phase)


def reduce_boxes(nb, nz, rows, columns):
    half = rows // 2
    return [
        pltpu.VMEM((2, nb, 2, rows, columns), BF),
        pltpu.VMEM((2, nb, rows, columns), BF),
        pltpu.VMEM((nb - 1, 2, half, columns), BF),
        pltpu.VMEM((nb, half, columns), BF),
        pltpu.VMEM((half, columns), BF),
        pltpu.VMEM((nb - 1, half, columns), BF),
        pltpu.VMEM((nz - 1, rows, columns // nz), BF),
    ]


def key_parts(span, block):
    low = max(0, (block - 1) * ROWS)
    high = min(span, (block + 2) * ROWS)
    if low <= ROWS:
        return [(0, high)]
    return [(0, ROWS), (low, high)]


def head_masks():
    lane = lax.broadcasted_iota(jnp.int32, (1, LANES), 1)
    return (lane < HD, lane >= HD)


def only(mask, block):
    return jnp.where(mask, block, jnp.zeros_like(block))


def make_bias(marks_ref, bias):
    span = bias.shape[0]
    for i in range(0, span, ROWS):
        part = slice(i, i + ROWS)
        distance = lax.broadcasted_iota(jnp.int32, (ROWS, span), 0) + i - lax.broadcasted_iota(jnp.int32, (ROWS, span), 1)
        near = jnp.where(jnp.abs(distance) <= W // 2, 0.0, NEGATIVE)
        near = jnp.where(marks_ref[part, 1:2] > 0.5, 0.0, near)
        bias[part, :] = jnp.where(marks_ref[part, 0:1] > 0.5, near, NEGATIVE)


def attend_local(refs, bias_ref, a_ref, lse_ref, tick):
    k_ref, v_ref, q_ref = refs
    span = q_ref.shape[0]
    masks = head_masks()
    query = q_ref[...] * jnp.asarray(HD ** (-0.5), BF)
    values_flip = v_ref[...].T
    for block in range(span // ROWS):
        tick(block)
        rows = slice(block * ROWS, (block + 1) * ROWS)
        parts = key_parts(span, block)
        flips = []
        for h in range(2):
            head_query = only(masks[h], query[rows])
            scored = [
                product_back(k_ref[lo:hi, :], head_query) + bias_ref[lo:hi, rows] for lo, hi in parts
            ]
            top = jnp.max(scored[0], axis=0, keepdims=True)
            for s in scored[1:]:
                top = jnp.maximum(top, jnp.max(s, axis=0, keepdims=True))
            weights = [jnp.exp(s - top) for s in scored]
            total = sum(jnp.sum(w, axis=0, keepdims=True) for w in weights)
            lse_ref[0, h : h + 1, rows] = top + jnp.log(total)
            mixed = sum(
                product(values_flip[h * HD : (h + 1) * HD, lo:hi], w.astype(BF))
                for (lo, hi), w in zip(parts, weights)
            )
            flips.append(mixed * (1.0 / total))
        a_ref[rows, :] = jnp.concatenate(flips, axis=0).T.astype(BF)


def attend_global(refs, qg_ref, marks_ref, place_ref, a_ref, lse_global_ref):
    kg_ref, vg_ref = refs
    masks = head_masks()
    query = qg_ref[...] * jnp.asarray(HD ** (-0.5), BF)
    stacked = jnp.concatenate([only(m, query) for m in masks], axis=0)
    scores = product_back(kg_ref[...], stacked) + jnp.where(marks_ref[:, 0:1] > 0.5, 0.0, NEGATIVE)
    top = jnp.max(scores, axis=0, keepdims=True)
    probs = jnp.exp(scores - top)
    total = jnp.sum(probs, axis=0, keepdims=True)
    lse_global_ref[...] = jnp.broadcast_to(top + jnp.log(total), (8, LANES))
    probs = (probs * (1.0 / total)).astype(BF)
    mixed = product_left(probs, vg_ref[...])
    global_out = jnp.where(masks[0], mixed[:NG], mixed[NG:]).astype(BF)
    global_rows = product(place_ref[...], global_out)
    is_global = marks_ref[:ROWS, 1:2] > 0.5
    a_ref[:ROWS, :] = jnp.where(is_global, global_rows, a_ref[:ROWS, :].astype(F32)).astype(BF)


def attention_backward(refs, qg_ref, bias_ref, marks_ref, place_ref, a_ref, da_ref, lse_ref, lse_global_ref,
                       back_refs, dqg_ref, sums_ref, dk_sum, dv_sum, tick):
    k_ref, v_ref, q_ref, kg_ref, vg_ref = refs
    dk_ref, dv_ref, dq_ref, dkg_ref, dvg_ref = back_refs
    span = q_ref.shape[0]
    masks = head_masks()
    scale = HD ** (-0.5)
    query = q_ref[...] * jnp.asarray(scale, BF)
    keys_flip = k_ref[...].T
    query_global = qg_ref[...] * jnp.asarray(scale, BF)
    stacked = jnp.concatenate([only(m, query_global) for m in masks], axis=0)
    adjoint_global = product_left(place_ref[...], da_ref[:ROWS, :]).astype(BF)
    adjoint_stacked = jnp.concatenate([only(m, adjoint_global) for m in masks], axis=0)
    scores = product_back(kg_ref[...], stacked) + jnp.where(marks_ref[:, 0:1] > 0.5, 0.0, NEGATIVE)
    probs = jnp.exp(scores - lse_global_ref[0, 0:1, :])
    prob_adjoint = product_back(vg_ref[...], adjoint_stacked)
    center = jnp.sum(probs * prob_adjoint, axis=0, keepdims=True)
    score_adjoint = (probs * (prob_adjoint - center)).astype(BF)
    mixed = product_left(score_adjoint, kg_ref[...]) * scale
    dqg_ref[...] = jnp.where(masks[0], mixed[:NG], mixed[NG:]).astype(BF)
    dkg_ref[...] = product(score_adjoint, stacked).astype(BF)
    dvg_ref[...] = product(probs.astype(BF), adjoint_stacked).astype(BF)
    first = jnp.where(marks_ref[:ROWS, 1:2] > 0.5, 0.0, da_ref[:ROWS, :].astype(F32)).astype(BF)
    adjoint = jnp.concatenate([first, da_ref[ROWS:, :]], axis=0)
    inner = adjoint.astype(F32) * a_ref[...].astype(F32)
    picker = (lax.broadcasted_iota(jnp.int32, (8, LANES), 0) == lax.div(lax.broadcasted_iota(jnp.int32, (8, LANES), 1), HD)).astype(F32)
    centers = lax.dot_general(
        picker, inner, (((1,), (1,)), ((), ())), preferred_element_type=F32, precision=lax.Precision.HIGHEST
    )
    dk_sum[...] = jnp.zeros_like(dk_sum)
    dv_sum[...] = jnp.zeros_like(dv_sum)
    for block in range(span // ROWS):
        tick(block)
        rows = slice(block * ROWS, (block + 1) * ROWS)
        parts = key_parts(span, block)
        flips = []
        for h in range(2):
            head_query = only(masks[h], query[rows])
            head_adjoint = only(masks[h], adjoint[rows])
            log_sum = lse_ref[0, h : h + 1, rows]
            center = centers[h : h + 1, rows]
            mixed = None
            for lo, hi in parts:
                s = product_back(k_ref[lo:hi, :], head_query) + bias_ref[lo:hi, rows]
                weights = jnp.exp(s - log_sum)
                prob_adjoint = product_back(v_ref[lo:hi, :], head_adjoint)
                score_adjoint = (weights * (prob_adjoint - center)).astype(BF)
                dv_sum[lo:hi, :] += product(weights.astype(BF), head_adjoint)
                dk_sum[lo:hi, :] += product(score_adjoint, head_query)
                part = product(keys_flip[h * HD : (h + 1) * HD, lo:hi], score_adjoint)
                mixed = part if mixed is None else mixed + part
            flips.append(mixed)
        dq_ref[rows, :] = (jnp.concatenate(flips, axis=0).T * scale).astype(BF)
    dk_ref[...] = dk_sum[...].astype(BF)
    dv_ref[...] = dv_sum[...].astype(BF)
    sums = [jnp.sum(r[...].astype(F32), axis=0, keepdims=True) for r in (dq_ref, dv_ref, dqg_ref, dvg_ref)]
    sums_ref[...] = jnp.concatenate(sums + [jnp.zeros((4, LANES), F32)], axis=0)


def gelu_and_slope(u):
    e = jnp.exp2(u * (u * (-0.5 * 1.4426950408889634)))
    t = 1.0 / (1.0 + (0.3275911 * 0.7071067811865476) * jnp.abs(u))
    tail = 0.5 * -1.453152027 + t * (0.5 * 1.061405429)
    tail = 0.5 * -0.284496736 + t * (0.5 * 1.421413741 + t * tail)
    tail = t * (0.5 * 0.254829592 + t * tail) * e
    phi = jnp.where(u >= 0.0, 1.0 - tail, tail)
    return u * phi, phi + u * e * 0.3989422804014327


def normalize(mixture):
    centered = mixture - jnp.mean(mixture, axis=-1, keepdims=True)
    spread = lax.rsqrt(jnp.mean(centered * centered, axis=-1, keepdims=True) + EPS_NORM)
    return centered * spread, spread


def normalize_back(adjoint, normal, spread, gain):
    scaled = adjoint * gain
    mean = jnp.mean(scaled, axis=-1, keepdims=True)
    along = jnp.mean(scaled * normal, axis=-1, keepdims=True)
    return spread * (scaled - mean - normal * along)


def kernel_params(collective=None, **more):
    if collective is not None:
        more.update(collective_id=collective, has_side_effects=True)
    return pltpu.CompilerParams(vmem_limit_bytes=61 * MIB, **more)


def dma(count):
    return pltpu.SemaphoreType.DMA((count,))


def still(*shape):
    return pl.BlockSpec(shape, lambda s: (0,) * len(shape), pipeline_mode=pl.Buffered(1))


def full_shape(nb, block, columns, *lead):
    return lead + (2, nb, 2, block, columns)


def everyone(spot):
    devices = spot.groups * spot.nz
    me = spot.g * spot.nz + spot.z
    ids = [lax.rem(me + i, devices) for i in range(1, devices)]
    return [(lax.div(i, spot.nz), lax.rem(i, spot.nz)) for i in ids]


def project_and_attend(mesh, low_in, low_rest, low_vectors, sequence, place, marks, parts):
    groups, depth = mesh.shape["grp"], mesh.shape["dp"]
    nb = groups // 4
    count, block, width = low_in.shape
    rest = low_rest.shape[0]
    span, columns = sequence.shape
    devices = groups * depth
    few = place.shape[1]
    pairs = H // 2
    total = (count + rest) * gather_copies(nb, depth) + depth - 1 + devices - 1
    lag = 3
    local_count = 3
    attend = lag + local_count
    project = attend + pairs
    glob = project + count - local_count
    together = 2
    steps = glob + pairs // together

    def slot(s):
        return 4 * s if s < attend else 4 * attend + 6 * (s - attend)

    def kernel(in_ref, rest_ref, vec_ref, seq_ref, place_ref, marks_ref, part_ref,
               full_ref, out_ref, up_ref, vec_full_ref, proj_ref, few_ref, a_ref, lse_ref, lse_global_ref, swapped_ref,
               weight, vec, proj, bias, send, recv, local):
        spot = Spot(groups, depth)
        sems = Sems(send, recv)
        pairs_of = [(in_ref.at[t], full_ref.at[t]) for t in range(count)]
        pairs_of += [(rest_ref.at[0], out_ref)] + [(rest_ref.at[1 + q], up_ref.at[q]) for q in range(rest - 1)]
        pieces = [GatherPiece(spot, sems, local.at[t], src, out) for t, (src, out) in enumerate(pairs_of)]
        swap = Swap(spot, sems, local.at[count + rest], part_ref, swapped_ref)
        own = pl.ds(pl.multiple_of(spot.z * width, LANES), width)
        mine = vec_full_ref.at[:, own]
        vec_local = pltpu.make_async_copy(vec_ref, mine, local.at[count + rest + 1])
        vec_sends = [sems.copy(vec_ref, mine, spot.at(z=spot.z_off(i))) for i in range(1, depth)]
        keep = [
            pltpu.make_async_copy(proj.at[t], proj_ref.at[t], local.at[count + rest + 2 + t]) for t in range(count - 1)
        ]
        step = pl.program_id(0)
        ticks = Ticks(4)
        times = slot_times(slot, count + rest)
        for t in range(local_count, count + rest):
            times[t] = [slot(t - 2) + 1, slot(t), slot(t + 2) + 1, slot(t + 4) + 2, slot(t + 5) + 3]
        ticks.add_all(timeline(pieces, times))
        for j in range(8):
            ticks.add(4 * (attend + 2 * j if j < 4 else project + j - 4) + 2, lambda j=j: swap.start(j, 8))

        @pl.when(step == 0)
        def _():
            greet(everyone(spot))
            vec_local.start()
            start_all(vec_sends)

        for c in range(4):
            ticks.here(c, 0, attend - 1)

        @pl.when(step == 0)
        def _():
            make_bias(marks_ref, bias)

        @pl.when(step == lag)
        def _():
            vec_local.wait()
            recv_all(vec_sends)
            send_done(vec_sends)
            pltpu.sync_copy(vec_full_ref, vec)

        def offset(row):
            index = lax.broadcasted_iota(jnp.int32, vec.shape, 0)
            return jnp.sum(jnp.where(index == row, vec[...].astype(F32), 0.0), axis=0, keepdims=True)

        for c in range(4):
            ticks.here(c, project, steps - 1)

        def project_one(t):
            pltpu.sync_copy(full_ref.at[t], weight)
            added = offset(jnp.where(t == 1, 1, jnp.where(t == 2, 0, jnp.where(t == 4, 4, 15))))

            def body(rows):
                matrix = weight[...].reshape(groups * block, columns)
                proj[t, rows, :] = (product(seq_ref[rows, :], matrix) + added).astype(BF)

            in_chunks(span, body)

        first_part = jnp.logical_and(step >= lag, step < attend)
        second_part = jnp.logical_and(step >= project, step < glob - 1)
        pl.when(jnp.logical_or(first_part, second_part))(
            lambda: project_one(jnp.where(step < attend, step - lag, step - project + local_count))
        )
        for t in range(count - 1):
            pl.when(step == (lag + t if t < local_count else project + t - local_count))(keep[t].start)

        @pl.when(step == glob - 1)
        def _():
            pltpu.sync_copy(full_ref.at[count - 1], weight)
            matrix = weight[...].reshape(groups * block, columns)
            rows = product_left(place_ref[...], seq_ref[:ROWS, :]).astype(BF)
            few_ref[...] = (product(rows, matrix) + offset(3)).astype(BF)

        @during(attend, project - 1)
        def _():
            lanes = pl.ds(pl.multiple_of((step - attend) * LANES, LANES), LANES)
            attend_local(
                [proj.at[i, :, lanes] for i in range(local_count)], bias, a_ref.at[:, lanes], lse_ref,
                lambda c: ticks.here(c, attend, project - 1),
            )

        @pl.when(step >= glob)
        def _():
            def one(i, carry):
                pair = (step - glob) * together + i
                lanes = pl.ds(pl.multiple_of(pair * LANES, LANES), LANES)
                attend_global(
                    [proj.at[i, :, lanes] for i in range(local_count, count - 1)], few_ref.at[:, lanes], marks_ref, place_ref,
                    a_ref.at[:, lanes], lse_global_ref.at[pair],
                )
                return carry

            lax.fori_loop(0, together, one, 0)

        @pl.when(step == steps - 1)
        def _():
            for copy in keep:
                copy.wait()
            swap.finish()

    at = lambda s: jnp.clip(s - attend, 0, pairs - 1)
    results = pl.pallas_call(
        kernel,
        grid=(steps,),
        in_specs=[ANYSPEC] * 3 + [still(span, columns), still(*place.shape), still(*marks.shape), ANYSPEC],
        out_specs=[ANYSPEC] * 5
        + [
            pl.BlockSpec((few, columns), lambda s: (0, 0)),
            pl.BlockSpec((span, columns), lambda s: (0, 0)),
            pl.BlockSpec((1, 8, span), lambda s: (at(s), 0, 0)),
            pl.BlockSpec((pairs, 8, LANES), lambda s: (0, 0, 0)),
            ANYSPEC,
        ],
        out_shape=[
            jax.ShapeDtypeStruct(full_shape(nb, block, columns, count), BF),
            jax.ShapeDtypeStruct(full_shape(nb, block, columns), BF),
            jax.ShapeDtypeStruct(full_shape(nb, block, columns, rest - 1), BF),
            jax.ShapeDtypeStruct((low_vectors.shape[0], columns), BF),
            jax.ShapeDtypeStruct((count - 1, span, columns), BF),
            jax.ShapeDtypeStruct((few, columns), BF),
            jax.ShapeDtypeStruct((span, columns), BF),
            jax.ShapeDtypeStruct((pairs, 8, span), F32),
            jax.ShapeDtypeStruct((pairs, 8, LANES), F32),
            jax.ShapeDtypeStruct(parts.shape, BF),
        ],
        scratch_shapes=[
            pltpu.VMEM(full_shape(nb, block, columns), BF),
            pltpu.VMEM((low_vectors.shape[0], columns), BF),
            pltpu.VMEM((count - 1, span, columns), BF),
            pltpu.VMEM((span, span), F32),
            dma(total),
            dma(total),
            dma(count + rest + 2 + count - 1),
        ],
        compiler_params=kernel_params(0),
        name="project_and_attend",
    )(low_in, low_rest, low_vectors, sequence, place, marks, parts)
    square = (groups * block, columns)
    full_in, full_out, full_up = results[:3]
    return (full_in.reshape((count,) + square), full_out.reshape(square), full_up.reshape((rest - 1,) + square)) + tuple(
        results[3:]
    )


def feed_forward(mesh, sequence, attended, full_out, full_up, shards, parts, vectors, hidden_bias, valid):
    groups, depth = mesh.shape["grp"], mesh.shape["dp"]
    nb = groups // 4
    span, columns = sequence.shape
    count, block, width = shards.shape
    devices = groups * depth
    total = count * gather_copies(nb, depth) + devices - 1
    steps = count + 3
    extra = FF // D

    def kernel(seq_ref, att_ref, wo_ref, up_ref, shard_ref, part_ref, vec_ref, hb_ref, valid_ref,
               full_ref, hid_ref, slope_ref, low_ref, normal_ref, spread_ref, layer_ref, feed_low_ref, sum_ref, sums_ref,
               first, low, normal, hidden, feed, weight, cot, send, recv, local):
        spot = Spot(groups, depth)
        sems = Sems(send, recv)
        pieces = [GatherPiece(spot, sems, local.at[t], shard_ref.at[t], full_ref.at[t]) for t in range(count)]
        swap = Swap(spot, sems, local.at[count], part_ref, cot)
        keep_low = pltpu.make_async_copy(low, low_ref, local.at[count + 1])
        keep_normal = pltpu.make_async_copy(normal, normal_ref, local.at[count + 2])
        keep_hidden = [
            pltpu.make_async_copy(hidden.at[q], hid_ref.at[q], local.at[count + 3 + q]) for q in range(count)
        ]
        keep_sum = pltpu.make_async_copy(feed, sum_ref, local.at[2 * count + 3])
        step = pl.program_id(0)

        @pl.when(step == 0)
        def _():
            greet(everyone(spot))

        ticks = Ticks(8)
        starts = [[0, 1, 2, 3], [8, 16, 24, 32], [10, 19, 28, 37], [18, 27, 36, 45], [25, 34, 44, 52]]
        ticks.add_all(timeline(pieces, [[starts[p][q] for p in range(5)] for q in range(count)]))
        for j, tick in enumerate((3, 5, 8, 9, 10, 11, 16, 17)):
            ticks.add(tick, lambda j=j: swap.start(j, 8))
        chunks = [slice(i, i + ROWS) for i in range(0, span, ROWS)]

        def work(first, last, offset, body):
            @during(first, last)
            def _():
                for c, rows in enumerate(chunks):
                    ticks.here(offset + c, first, last)
                    body(rows)

        def idle(first, last, offset):
            for c in range(len(chunks)):
                ticks.here(offset + c, first, last)

        def norm(rows):
            mixture = seq_ref[rows, :].astype(F32) + product(att_ref[rows, :], wo_ref[...]) + vec_ref[2:3, :]
            centered, spread = normalize(mixture)
            out = centered * vec_ref[6 + extra : 7 + extra, :] + vec_ref[7 + extra : 8 + extra, :]
            first[rows, :] = out
            low[rows, :] = out.astype(BF)
            feed[rows, :] = jnp.broadcast_to(vec_ref[5 + extra : 6 + extra, :], (ROWS, columns))
            normal[rows, :] = centered.astype(BF)
            spread_ref[rows, :] = jnp.broadcast_to(spread, (ROWS, LANES))

        def up(rows):
            q = step - 1
            u = product(low[rows, :], up_ref[0]) + hb_ref[pl.ds(q, 1), :]
            act, slope = gelu_and_slope(u)
            hidden[q, rows, :] = act.astype(BF)
            slope_ref[0, rows, :] = slope.astype(BF)

        def down(rows):
            part = product(hidden[step - 3, rows, :], weight[...].reshape(groups * block, columns))
            feed[rows, :] += part

        work(0, 0, 0, norm)

        @pl.when(step == 0)
        def _():
            keep_low.start()
            keep_normal.start()

        idle(0, 2, 4)
        work(1, count, 0, up)
        for q in range(count):
            pl.when(step == q + 1)(keep_hidden[q].start)
        idle(count + 1, steps - 1, 0)
        for q in range(count):

            @pl.when(step == q + 3)
            def _(q=q):
                ticks.here(4, q + 3, q + 3)
                pltpu.sync_copy(full_ref.at[q], weight)

        @during(3, steps - 1)
        def _():
            for c, rows in enumerate(chunks):
                if c:
                    ticks.here(4 + c, 3, steps - 1)
                down(rows)


        @pl.when(step == steps - 1)
        def _():
            swap.finish()
            sums_ref[...] = jnp.zeros_like(sums_ref)
            pieces_of = span // devices

            def body(rows):
                part = pl.ds(rows.start // pieces_of, ROWS // pieces_of)
                mask = valid_ref[rows, 0:1]
                cotangent = cot[part].reshape(ROWS, columns).astype(F32) * mask
                gain = vec_ref[8 + extra : 9 + extra, :]
                mixture = first[rows, :] + feed[rows, :]
                centered, spread = normalize(mixture)
                layer_ref[rows, :] = ((centered * gain + vec_ref[9 + extra : 10 + extra, :]) * mask).astype(BF)
                back = normalize_back(cotangent, centered, spread, gain)
                back_low = back.astype(BF)
                feed[rows, :] = back
                feed_low_ref[rows, :] = back_low
                sums_ref[0:1, :] += jnp.sum(back_low.astype(F32), axis=0, keepdims=True)
                sums_ref[1:2, :] += jnp.sum(cotangent * centered, axis=0, keepdims=True)
                sums_ref[2:3, :] += jnp.sum(cotangent, axis=0, keepdims=True)

            in_chunks(span, body)
            keep_sum.start()
            keep_low.wait()
            keep_normal.wait()
            for copy in keep_hidden:
                copy.wait()
            keep_sum.wait()

    matrix = lambda kind: jax.ShapeDtypeStruct((span, columns), kind)
    stack = jax.ShapeDtypeStruct((count, span, columns), BF)
    by_q = pl.BlockSpec((1, span, columns), lambda s: (jnp.clip(s - 1, 0, count - 1), 0, 0))
    results = pl.pallas_call(
        kernel,
        grid=(steps,),
        in_specs=[
            still(span, columns), still(span, columns), still(*full_out.shape), by_q, ANYSPEC, ANYSPEC,
            still(*vectors.shape), still(*hidden_bias.shape), still(*valid.shape),
        ],
        out_specs=[ANYSPEC, ANYSPEC, by_q, ANYSPEC, ANYSPEC]
        + [pl.BlockSpec((span, LANES), lambda s: (0, 0))]
        + [pl.BlockSpec((span, columns), lambda s: (0, 0))] * 2
        + [ANYSPEC, pl.BlockSpec((8, columns), lambda s: (0, 0))],
        out_shape=[
            jax.ShapeDtypeStruct(full_shape(nb, block, columns, count), BF), stack, stack, matrix(BF), matrix(BF),
            jax.ShapeDtypeStruct((span, LANES), F32), matrix(BF), matrix(BF), matrix(F32),
            jax.ShapeDtypeStruct((8, columns), F32),
        ],
        scratch_shapes=[
            pltpu.VMEM((span, columns), F32),
            pltpu.VMEM((span, columns), BF),
            pltpu.VMEM((span, columns), BF),
            pltpu.VMEM((count, span, columns), BF),
            pltpu.VMEM((span, columns), F32),
            pltpu.VMEM(full_shape(nb, block, columns), BF),
            pltpu.VMEM(parts.shape, BF),
            dma(total),
            dma(total),
            dma(2 * count + 4),
        ],
        compiler_params=kernel_params(1),
        name="feed_forward",
    )(sequence, attended, full_out, full_up, shards, parts, vectors, hidden_bias, valid)
    return (results[0].reshape(count, groups * block, columns),) + tuple(results[1:])


def feed_backward(mesh, feed_low, low, hidden, slope, full_up, full_down, sum_adjoint, attended, full_out, normal, spread,
                  gain, parts):
    groups, depth = mesh.shape["grp"], mesh.shape["dp"]
    nb = groups // 4
    span, columns = feed_low.shape
    count = hidden.shape[0]
    block, width = columns // groups, columns // depth
    devices = groups * depth
    half = columns // 2
    total = count * reduce_copies(nb, depth) + devices - 1
    work = 3 * count
    steps = work + 2
    boxes = [reduce_boxes(nb, depth, block, columns) for _ in range(count)]
    per = len(boxes[0])

    def kernel(feed_ref, low_ref, hid_ref, slope_ref, up_ref, down_ref, sum_ref, att_ref, wo_ref, normal_ref, spread_ref,
               gain_ref, part_ref,
               change_ref, hb_ref, mix_ref, own_ref, swapped_ref, out_change_ref, att_back_ref, sums_ref,
               back_low, norm, branch, send, recv, local, *box_refs):
        spot = Spot(groups, depth)
        sems = Sems(send, recv)
        tiles = [box_refs[q * per] for q in range(count)]

        def finish(q):
            def store(value):
                own_ref[q] = value

            return store

        pieces = [
            ReducePiece(spot, sems, None, None, width, box_refs[q * per : (q + 1) * per], finish(q)) for q in range(count)
        ]
        swap = Swap(spot, sems, local.at[0], part_ref, swapped_ref)
        keep = pltpu.make_async_copy(norm, mix_ref, local.at[1])
        fetch = pltpu.make_async_copy(sum_ref, norm, local.at[2])
        step = pl.program_id(0)
        ticks = Ticks(4)
        starts = [[3, 7, 11, 15], [7, 19, 27, 35], [17, 25, 33, 41], [22, 30, 38, 46], [31, 39, 47, 53]]
        ticks.add_all(timeline(pieces, [[starts[p][q] for p in range(5)] for q in range(count)]))
        for j in range(8):
            ticks.add(4 * (j + 2), lambda j=j: swap.start(j, 8))
        chunks = [slice(i, i + ROWS) for i in range(0, span, ROWS)]

        def work_on(first, last, body):
            for c, rows in enumerate(chunks):
                if c == len(chunks) // 2:
                    ticks.here(1, first, last)
                body(rows)
            ticks.here(2, first, last)

        @pl.when(step == 0)
        def _():
            greet(everyone(spot))
            fetch.start()

        ticks.here(0, 0, steps - 1)

        for q in range(count):

            @pl.when(step == q)
            def _(q=q):
                value = product_left(hid_ref[0], feed_ref[...]).astype(BF)
                tiles[q][...] = value.reshape(full_shape(nb, block, columns))

        pl.when(step == count)(fetch.wait)

        for c in (1, 2):
            ticks.here(c, 0, count - 1)

        @during(count, work - 1)
        def _():
            hb_ref[...] = jnp.zeros_like(hb_ref)

            def body(rows):
                value = product_back(feed_ref[rows, :], down_ref[0]) * slope_ref[0, rows, :].astype(F32)
                value = value.astype(BF)
                back_low[rows, :] = value
                hb_ref[0] += jnp.broadcast_to(jnp.sum(value.astype(F32), axis=0, keepdims=True), (8, half))
                norm[rows, :] += product_back(value, up_ref[0])

            work_on(count, work - 1, body)
            change_ref[0] = product_left(low_ref[...], back_low[...]).astype(BF)

        @pl.when(step == work)
        def _():
            sums_ref[...] = jnp.zeros_like(sums_ref)

            def body(rows):
                adjoint = norm[rows, :]
                centered = normal_ref[rows, :].astype(F32)
                back = normalize_back(adjoint, centered, spread_ref[rows, 0:1], gain_ref[0:1, :])
                back_branch = back.astype(BF)
                norm[rows, :] = back
                branch[rows, :] = back_branch
                sums_ref[0:1, :] += jnp.sum(back_branch.astype(F32), axis=0, keepdims=True)
                sums_ref[1:2, :] += jnp.sum(adjoint * centered, axis=0, keepdims=True)
                sums_ref[2:3, :] += jnp.sum(adjoint, axis=0, keepdims=True)
                att_back_ref[rows, :] = product_back(back_branch, wo_ref[...]).astype(BF)

            work_on(work, work, body)
            keep.start()
            out_change_ref[...] = product_left(att_ref[...], branch[...]).astype(BF)

        ticks.here(3, 0, work)
        for c in range(1, 4):
            ticks.here(c, work + 1, steps - 1)

        @pl.when(step == steps - 1)
        def _():
            keep.wait()
            swap.finish()

    at = lambda s: jnp.clip(s - count, 0, 2 * count - 1)
    by_half = pl.BlockSpec((1, span, half), lambda s: (lax.div(at(s), 2), 0, lax.rem(at(s), 2)))
    whole = lambda *dims: pl.BlockSpec(dims, lambda s: (0,) * len(dims))
    return pl.pallas_call(
        kernel,
        grid=(steps,),
        in_specs=[
            still(span, columns), still(span, columns),
            pl.BlockSpec((1, span, columns), lambda s: (jnp.minimum(s, count - 1), 0, 0)),
            by_half, by_half,
            pl.BlockSpec((1, half, columns), lambda s: (lax.div(at(s), 2), lax.rem(at(s), 2), 0)),
            ANYSPEC, still(span, columns), still(columns, columns), still(span, columns), still(span, LANES),
            still(8, columns), ANYSPEC,
        ],
        out_specs=[
            by_half,
            pl.BlockSpec((1, 8, half), lambda s: (lax.div(at(s), 2), 0, lax.rem(at(s), 2))),
            ANYSPEC, whole(count, block, width), ANYSPEC, whole(columns, columns), whole(span, columns), whole(8, columns),
        ],
        out_shape=[
            jax.ShapeDtypeStruct((count, columns, columns), BF),
            jax.ShapeDtypeStruct((count, 8, columns), F32),
            jax.ShapeDtypeStruct((span, columns), F32),
            jax.ShapeDtypeStruct((count, block, width), F32),
            jax.ShapeDtypeStruct(parts.shape, BF),
            jax.ShapeDtypeStruct((columns, columns), BF),
            jax.ShapeDtypeStruct((span, columns), BF),
            jax.ShapeDtypeStruct((8, columns), F32),
        ],
        scratch_shapes=[
            pltpu.VMEM((span, half), BF),
            pltpu.VMEM((span, columns), F32),
            pltpu.VMEM((span, columns), BF),
            dma(total),
            dma(total),
            dma(3),
        ]
        + [box for some in boxes for box in some],
        compiler_params=kernel_params(2),
        name="feed_backward",
    )(feed_low, low, hidden, slope, full_up, full_down, sum_adjoint, attended, full_out, normal, spread, gain, parts)


def attend_back_and_reduce(mesh, projected, query_global, marks, place, attended, attended_adjoint, log_sums, log_sums_global,
                           changes, parts, full_in, sequence, mixture_adjoint, hidden_sums, feed_sums, norm_sums, order):
    groups, depth = mesh.shape["grp"], mesh.shape["dp"]
    nb = groups // 4
    span, columns = sequence.shape
    pairs = H // 2
    count = full_in.shape[0]
    few = query_global.shape[0]
    block, width = columns // groups, columns // depth
    devices = groups * depth
    views = [c.reshape((-1,) + full_shape(nb, block, columns)) for c in changes]
    where = [(i, t) for i, v in enumerate(views) for t in range(v.shape[0])]
    early = len(where)
    given = len(views)
    vec_rows = 16
    extra = hidden_sums.shape[0]
    total = (early + count) * reduce_copies(nb, depth) + devices - 1 + depth - 1 + groups - 1
    late_starts = [4 * (pairs + t) + 3 for t in range(count)]
    late_times = [[m, m + 3, m + 9, m + 12, m + 16] for m in late_starts]
    steps = late_times[-1][-1] // 4 + 1
    boxes = [reduce_boxes(nb, depth, block, columns) for _ in range(max(early + 1, count))]
    per = len(boxes[0])

    def kernel(*refs):
        stack_ref, few_ref, marks_ref, place_ref, a_ref, da_ref, lse_ref, lse_global_ref = refs[:8]
        change_refs, refs = refs[8 : 8 + given], refs[8 + given :]
        part_ref, weight_ref, seq_ref, mix_ref, hidden_ref, feed_ref, norm_ref = refs[:7]
        own_refs, own_in_ref, vec_out, grad_ref, swapped_ref = refs[7 : 7 + given], *refs[7 + given : 11 + given]
        refs = refs[11 + given :]
        bias, back, dqg, sums, dk_sum, dv_sum, grad, vec, vec_z, vec_g, send, recv, local, free = refs[:14]
        box_refs = refs[14:]
        spot = Spot(groups, depth)
        sems = Sems(send, recv)

        def finish(ref, i):
            def store(value):
                ref[i] = value

            return store

        box = lambda i: box_refs[i * per : (i + 1) * per]
        pieces = [
            ReducePiece(spot, sems, local.at[i], change_refs[v].at[t], width, box(i), finish(own_refs[v], t))
            for i, (v, t) in enumerate(where)
        ]
        late_box = [early] + list(range(early)) + list(range(early + 1, count))
        late = [
            ReducePiece(spot, sems, None, None, width, box(late_box[t]), finish(own_in_ref, int(order[t]))) for t in range(count)
        ]
        tiles = [box_refs[late_box[t] * per] for t in range(count)]
        swap = Swap(spot, sems, local.at[early], part_ref, swapped_ref)
        fetch = pltpu.make_async_copy(mix_ref, grad, local.at[early + 1])
        keep = pltpu.make_async_copy(back.at[0], grad_ref, local.at[early + 2])
        part = lambda zz: pl.ds(pl.multiple_of(zz * width, LANES), width)
        first = [
            sems.copy(vec.at[:, part(spot.z_off(i))], vec_z.at[i - 1], spot.at(z=spot.z_off(i)))
            for i in range(1, depth)
        ]
        second = [
            sems.copy(vec_g.at[spot.g], vec_g.at[spot.g], (lax.rem(spot.g + i, groups), spot.z))
            for i in range(1, groups)
        ]
        step = pl.program_id(0)
        ticks = Ticks(4)
        ticks.add_all(
            timeline(pieces, [[max(0, 5 * t - 3), 5 * t + 2, 5 * t + 6, 5 * t + 9, 5 * t + 13] for t in range(early)])
        )
        for j, tick in enumerate((1, 5, 9, 13, 17, 29, 32, 35)):
            ticks.add(tick, lambda j=j: swap.start(j, 8))

        def freed():
            for target in spot.neighbours():
                pl.semaphore_signal(free, inc=1, device_id=target, device_id_type=MESH)

        ticks.add(5 * (early - 1) + 13, freed)
        ticks.add(late_starts[1], lambda: pl.semaphore_wait(free, len(spot.neighbours())))
        ticks.add_all(timeline(late, late_times))

        @pl.when(step == 0)
        def _():
            greet(everyone(spot))
            fetch.start()
            make_bias(marks_ref, bias)

        @pl.when(step < pairs)
        def _():
            lanes = pl.ds(pl.multiple_of(step * LANES, LANES), LANES)
            attention_backward(
                [stack_ref.at[i] for i in range(5)], few_ref, bias, marks_ref, place_ref,
                a_ref, da_ref, lse_ref, lse_global_ref,
                [back.at[i, :, lanes] for i in range(5)], dqg.at[:, lanes], sums.at[:, lanes], dk_sum, dv_sum,
                lambda c: ticks.here(c, 0, pairs - 1),
            )

        @pl.when(step == pairs)
        def _():
            fetch.wait()
            vec[...] = jnp.zeros_like(vec)
            vec[0:2, :] = sums[0:2, :]
            vec[2:3, :] = norm_ref[0:1, :]
            vec[3:5, :] = sums[2:4, :]
            vec[5 : 5 + extra, :] = hidden_ref[...]
            vec[5 + extra : 6 + extra, :] = feed_ref[0:1, :]
            vec[6 + extra : 8 + extra, :] = norm_ref[1:3, :]
            vec[8 + extra : 10 + extra, :] = feed_ref[1:3, :]
            start_all(first)

        ticks.here(0, pairs, steps - 1)
        ticks.here(1, pairs, steps - 1)

        for t in range(count - 1):

            @pl.when(step == pairs + t)
            def _(t=t):
                value = product_left(seq_ref[...], back[t]).astype(BF)
                tiles[t][...] = value.reshape(full_shape(nb, block, columns))

        @during(pairs, pairs + count - 2)
        def _():
            def body(rows):
                grad[rows, :] += product_back(back[step - pairs, rows, :], weight_ref[0])

            in_chunks(span, body)

        @pl.when(step == pairs + count - 1)
        def _():
            rows = product_left(place_ref[...], seq_ref[:ROWS, :]).astype(BF)
            value = product_left(rows, dqg[...]).astype(BF)
            tiles[count - 1][...] = value.reshape(full_shape(nb, block, columns))
            extra = product_back(dqg[...], weight_ref[0])
            grad[:ROWS, :] += lax.dot_general(
                place_ref[...].astype(F32), extra, (((1,), (0,)), ((), ())),
                precision=lax.Precision.HIGHEST, preferred_element_type=F32,
            )
            back[0] = grad[...].astype(BF)
            keep.start()

        ticks.here(2, pairs, steps - 1)
        ticks.here(3, pairs, steps - 1)

        @pl.when(step == pairs + 1)
        def _():
            recv_all(first)
            mine = vec[:, part(spot.z)]
            for i in range(depth - 1):
                mine = mine + vec_z[i]
            vec_g[spot.g] = mine
            start_all(second)

        @pl.when(step == steps - 1)
        def _():
            recv_all(second)
            whole = vec_g[0]
            for i in range(1, groups):
                whole = whole + vec_g[i]
            vec_out[...] = whole
            send_done(first)
            send_done(second)
            keep.wait()
            swap.finish()

    at = lambda s: jnp.minimum(s, pairs - 1)
    whole = lambda *dims: pl.BlockSpec(dims, lambda s: (0,) * len(dims))
    column = lambda rows: pl.BlockSpec((rows, LANES), lambda s: (0, at(s)))
    return pl.pallas_call(
        kernel,
        grid=(steps,),
        in_specs=[
            pl.BlockSpec((5, span, LANES), lambda s: (0, 0, at(s))),
            column(few), still(*marks.shape), still(*place.shape), column(span), column(span),
            pl.BlockSpec((1, 8, span), lambda s: (at(s), 0, 0)),
            pl.BlockSpec((1, 8, LANES), lambda s: (at(s), 0, 0)),
        ]
        + [ANYSPEC] * (given + 1)
        + [
            pl.BlockSpec((1, columns, columns), lambda s: (jnp.clip(s - pairs, 0, count - 1), 0, 0)),
            still(span, columns), ANYSPEC, still(*hidden_sums.shape), still(*feed_sums.shape), still(*norm_sums.shape),
        ],
        out_specs=[whole(v.shape[0], block, width) for v in views]
        + [whole(count, block, width), whole(vec_rows, width), ANYSPEC, ANYSPEC],
        out_shape=[jax.ShapeDtypeStruct((v.shape[0], block, width), F32) for v in views]
        + [
            jax.ShapeDtypeStruct((count, block, width), F32),
            jax.ShapeDtypeStruct((vec_rows, width), F32),
            jax.ShapeDtypeStruct((span, columns), BF),
            jax.ShapeDtypeStruct(parts.shape, BF),
        ],
        scratch_shapes=[
            pltpu.VMEM((span, span), F32),
            pltpu.VMEM((5, span, columns), BF),
            pltpu.VMEM((few, columns), BF),
            pltpu.VMEM((8, columns), F32),
            pltpu.VMEM((span, LANES), F32),
            pltpu.VMEM((span, LANES), F32),
            pltpu.VMEM((span, columns), F32),
            pltpu.VMEM((vec_rows, columns), F32),
            pltpu.VMEM((depth - 1, vec_rows, width), F32),
            pltpu.VMEM((groups, vec_rows, width), F32),
            dma(total),
            dma(total),
            dma(early + 3),
            pltpu.SemaphoreType.REGULAR,
        ]
        + [box for some in boxes for box in some],
        compiler_params=kernel_params(3),
        name="attend_back_and_reduce",
    )(projected, query_global, marks, place, attended, attended_adjoint, log_sums, log_sums_global, *views, parts, full_in,
      sequence, mixture_adjoint, hidden_sums, feed_sums, norm_sums)


def up_parts(matrix, ratio, parts):
    rows, columns = matrix.shape
    r = columns // (ratio * parts)
    return matrix.reshape(rows, ratio, parts, r).transpose(2, 0, 1, 3).reshape(parts, rows, ratio * r)


def up_whole(stack, ratio):
    parts, rows, columns = stack.shape
    r = columns // ratio
    return stack.reshape(parts, rows, ratio, r).transpose(1, 2, 0, 3).reshape(rows, parts * columns)


def per_device(mesh, tokens, out_cotangent, lengths, places, deal, in_weights, out_weight, up_weight, down_weight, vectors,
               first_in, first_out, first_up, first_down, first_vectors,
               second_in, second_out, second_up, second_down, second_vectors):
    groups, depth = mesh.shape["grp"], mesh.shape["dp"]
    ratio = groups // depth
    devices = groups * depth
    span = tokens.shape[1]
    quarters = FF // D
    me = lax.axis_index(("grp", "dp"))
    ids = jnp.arange(devices, dtype=jnp.int32)
    inverse = jnp.sum(jnp.where(deal[None, :] == ids[:, None], ids[None, :], 0), axis=1)
    length = lengths[me]
    spots = places[me]
    sequence = tokens[0]
    order = np.array([1, 2, 0, 4, 5, 3])

    low_in = jnp.stack([in_weights[i] for i in order]).astype(BF)
    low_rest = jnp.concatenate([out_weight.astype(BF)[None], up_parts(up_weight.astype(BF), ratio, quarters)])
    low_down = down_weight.astype(BF).reshape(quarters, -1, down_weight.shape[1])
    nv = vectors.shape[0]
    low_vectors = jnp.pad(vectors, ((0, 16 - nv), (0, 0))).astype(BF)

    positions = jnp.arange(span, dtype=jnp.int32)
    is_global = jnp.any(positions[:, None] == spots[None, :], axis=1)
    lane = jnp.arange(LANES)[None, :]
    marks = jnp.where(lane == 0, (positions < length)[:, None], (lane == 1) & is_global[:, None]).astype(F32)
    place = (positions[:ROWS, None] == spots[None, :]).astype(BF)
    shape_parts = (devices, span // devices, D)

    (full_in, full_out, full_up, full_vectors, projected, query_global, attended, log_sums, log_sums_global,
     cotangent_parts) = project_and_attend(
        mesh, low_in, low_rest, low_vectors, sequence, place, marks, out_cotangent.reshape(shape_parts)
    )
    vector_rows = full_vectors.astype(F32)
    hidden_bias = vector_rows[5 : 5 + quarters].reshape(groups, quarters, -1).transpose(1, 0, 2).reshape(quarters, D)
    cotangent_parts = cotangent_parts.at[deal].get(mode="promise_in_bounds")
    full_down, hidden, slope, first_low, normal_one, spread_one, layer_out, feed_low, sum_adjoint, feed_sums = feed_forward(
        mesh, sequence, attended, full_out, full_up, low_down, cotangent_parts, vector_rows, hidden_bias, marks
    )
    gain_one = jnp.broadcast_to(vector_rows[6 + quarters][None], (8, D))
    up_change, hidden_sums, mixture_adjoint, part_down, layer_parts, out_change, attended_adjoint, norm_sums = feed_backward(
        mesh, feed_low, first_low, hidden, slope, full_up, full_down, sum_adjoint, attended, full_out, normal_one, spread_one,
        gain_one, layer_out.reshape(shape_parts)
    )
    layer_parts = layer_parts.at[inverse].get(mode="promise_in_bounds")
    hidden_bias_change = hidden_sums[:, 0].reshape(quarters, groups, -1).transpose(1, 0, 2).reshape(quarters, D)
    part_up, part_out, part_in, part_vectors, token_gradient, layer_mine = attend_back_and_reduce(
        mesh, projected, query_global, marks, place, attended, attended_adjoint, log_sums, log_sums_global,
        (up_change, out_change), layer_parts, full_in, sequence, mixture_adjoint, hidden_bias_change, feed_sums, norm_sums,
        order
    )

    step_count = jnp.float32(STEP)
    fix_first = 1.0 - jnp.power(jnp.float32(BETA_FIRST), step_count)
    fix_second = 1.0 - jnp.power(jnp.float32(BETA_SECOND), step_count)

    def adam(weight, gradient, moment, square, decay):
        return adam_update(weight, gradient, moment, square, decay, fix_first, fix_second)

    part_up = up_whole(part_up, ratio)
    part_out = part_out[0]
    part_down = part_down.reshape(down_weight.shape)
    update_in, moment_in, square_in = adam(in_weights, part_in, first_in, second_in, WEIGHT_DECAY)
    update_out, moment_out, square_out = adam(out_weight, part_out, first_out, second_out, WEIGHT_DECAY)
    update_up, moment_up, square_up = adam(up_weight, part_up, first_up, second_up, WEIGHT_DECAY)
    update_down, moment_down, square_down = adam(down_weight, part_down, first_down, second_down, WEIGHT_DECAY)
    update_vectors, moment_vectors, square_vectors = adam(vectors, part_vectors[:nv], first_vectors, second_vectors, 0.0)
    return (
        layer_mine.reshape(tokens.shape), token_gradient[None],
        update_in, update_out, update_up, update_down, update_vectors,
        moment_in, moment_out, moment_up, moment_down, moment_vectors,
        square_in, square_out, square_up, square_down, square_vectors,
    )


def solution(mesh):
    sequences = P(("grp", "dp"), None, None)
    stack, matrix, rows = P(None, "grp", "dp"), P("grp", "dp"), P(None, "dp")
    packed = (stack, matrix, matrix, matrix, rows)
    return jax.shard_map(
        lambda *arrays: per_device(mesh, *arrays),
        mesh=mesh,
        in_specs=(sequences, sequences, P(), P(), P()) + packed * 3,
        out_specs=(sequences, sequences) + packed * 3,
        check_vma=False,
    )
```

time: 1190 us -> 593 us (0.50)
  Pallas kernels: 0 us -> 548 us
  matrix products: 466 us -> 0 us
  waiting for transfers between devices: 228 us -> 0 us
  other arithmetic: 195 us -> 13.5 us
  local copies, waits for them, and re-layouts: 157 us -> 21.4 us
  blocking collectives: 95 us -> 0 us
  starting transfers between devices: 18.8 us -> 0 us
  between operations: 17.7 us -> 1.37 us
    pallas_call x0 -> x4, Pallas kernels: none -> 548 us  [the longest x1 183 us: attend_back_and_reduce(): pl.pallas_call(kernel, grid=(steps,), in_specs=[pl.BlockSpec((5, span, LA...]
    dot_general x56 -> x0, matrix products: 460 us -> none  [the longest x9 96.7 us: product(): return jnp.dot(left_side, right_side, preferred_element_type=jnp.float32)]
    all_to_all x4 -> x0, waiting for transfers between devices: 118 us -> none  [the longest x1 46.1 us: per_device(): lax.all_to_all(tokens, ('grp', 'dp'), split_axis=1, concat_axis=0, tiled=...]
    all_gather x2 -> x0, blocking collectives: 67.8 us -> none  [the longest x1 52.3 us: per_device(): lax.all_gather(low_vectors, 'dp', axis=1, tiled=True)]
    convert_element_type x13 -> x5, other arithmetic: 69.1 us -> 4.02 us  [the longest x1 1.39 us: per_device(): vector_rows = full_vectors.astype(F32)]
    reduce_scatter x9 -> x0, waiting for transfers between devices: 56.8 us -> none  [the longest x1 33.4 us: per_device(): lax.psum_scatter(part_in.astype(jnp.bfloat16), 'dp', scatter_dimension=2,...]
    all_gather x7 -> x0, waiting for transfers between devices: 50.9 us -> none  [the longest x1 37.5 us: per_device(): lax.all_gather(low_in, 'dp', axis=2, tiled=True)]
    reduce_sum x12 -> x1, other arithmetic: 50.3 us -> 0.11 us  [per_device(): jnp.sum(jnp.where(deal[None, :] == ids[:, None], ids[None, :], 0), axis=1)]
  transfers between devices with their start and end apart: 20 -> 0, of which waited for: 7 -> 0; matrix products, arithmetic and copies ran while one was open for 61% -> 0% of each run, Pallas kernels for 0% -> 0%
where the time goes in v1:
time: 593 us; the launch traced here: 585 us
  Pallas kernels  548 us (92%)
  local copies, waits for them, and re-layouts  21.4 us (4%)
  other arithmetic  13.5 us (2%)
    pallas_call x1, Pallas kernels, attend_back_and_reduce(): pl.pallas_call(kernel, grid=(steps,), in_specs=[pl.BlockSpec((5, span, LA...  183 us
    pallas_call x1, Pallas kernels, project_and_attend(): pl.pallas_call(kernel, grid=(steps,), in_specs=[ANYSPEC] * 3 + [still(spa...  151 us
    pallas_call x1, Pallas kernels, feed_backward(): pl.pallas_call(kernel, grid=(steps,), in_specs=[still(span, columns), sti...  117 us
    pallas_call x1, Pallas kernels, feed_forward(): pl.pallas_call(kernel, grid=(steps,), in_specs=[still(span, columns), sti...  97.7 us

profile of v1, /device:TPU:0, one launch (start us, length us, event | category | flops | bytes accessed | tf_op | source)
XLA Modules:
  0.0 584.7 jit_solution(1135310129964935579)
XLA Ops:
  0.7 0.7 copy-done
  1.5 1.2 dynamic_slice.7
  2.8 0.6 iota_compare_fusion.2
  3.4 1.1 select_convert_fusion.marks_ref.valid_ref.refs_2_
  4.6 0.7 compare_convert_fusion.place_ref.refs_3_
  5.3 1.2 convert.14
  6.5 0.8 pad_maximum_fusion.in_ref
  8.0 0.8 pad_maximum_fusion.1.rest_ref
  8.7 0.6 pad.5.vec_ref
  9.3 151.3 %project_and_attend.1 = (bf16[6,2,2,2,128,1024]{5,4,3,2,1,0:T(8,128)(2,1)}, bf16[2,2,2,128,1024]{4,3,2,1,0:T(8,128)(2,1)}, bf16[4,2,2,2,128,1024]{5,4,3,2,1,0:T(...) custom-call(bf16[6,128,256]{2,1,0:T(8,128)(2,1)} %pad_maximum_fusion, ...), custom_call_target="tpu_custom_call" | custom-call | tf_op jit(solution)/shard_map/project_and_attend/pallas_call | solution.py:658
  160.7 0.8 slice.52
  161.5 0.6 copy.51
  162.1 1.4 convert_element_type.27.vec_ref
  163.5 3.6 gather_fusion
  167.1 0.7 convert_element_type.26
  167.9 97.7 %feed_forward.1 = (bf16[4,2,2,2,128,1024]{5,4,3,2,1,0:T(8,128)(2,1)}, bf16[4,1024,1024]{2,1,0:T(8,128)(2,1)}, bf16[4,1024,1024]{2,1,0:T(8,128)(2,1)}, bf16[1024,...) custom-call(bf16[1024,1024]{1,0:T(8,128)(2,1)} %bitcast.54, ...), custom_call_target="tpu_custom_call" | custom-call | tf_op jit(solution)/shard_map/feed_forward/pallas_call | solution.py:829
  265.6 0.7 slice.53
  266.3 0.6 broadcast_in_dim.58.gain_ref
  267.0 116.8 %feed_backward.1 = (bf16[4,1024,1024]{2,1,0:T(8,128)(2,1)}, f32[4,8,1024]{2,1,0:T(8,128)}, f32[1024,1024]{1,0:T(8,128)}, f32[4,128,256]{2,1,0:T(8,128)}, bf16[32...) custom-call(bf16[1024,1024]{1,0:T(8,128)(2,1)} %get-tuple-element.58.feed_r, ...), custom_call_target="tpu_custom_call" | custom-call | tf_op jit(solution)/shard_map/feed_backward/pallas_call | solution.py:978
  383.9 3.6 gather_fusion.1
  387.5 0.9 slice.42
  388.4 0.6 reshape.131.refs_14_
  389.1 182.5 %attend_back_and_reduce.1 = (f32[4,128,256]{2,1,0:T(8,128)}, f32[1,128,256]{2,1,0:T(8,128)}, f32[6,128,256]{2,1,0:T(8,128)}, f32[16,256]{1,0:T(8,128)}, bf16[102...) custom-call(bf16[5,1024,1024]{2,1,0:T(8,128)(2,1)} %get-tuple-element.51.refs_0_, ...), custom_call_target="tpu_custom_call" | custom-call | tf_op jit(solution)/shard_map/attend_back_and_reduce/pallas_call | solution.py:1182
  571.6 1.4 reshape.133
  573.6 1.4 multiply_add_fusion.2
  576.1 1.7 multiply_add_fusion
  577.8 0.8 multiply_add_fusion.3
  578.6 0.6 multiply_add_fusion.4
  579.2 1.4 multiply_add_fusion.1
  580.6 1.3 copy.56
  581.9 1.0 copy-done.5
  583.0 1.3 copy.57
  (69 shorter events, 2.6 us)
Async XLA Ops:
  0.7 0.7 copy-start
  0.7 6.7 %copy-start.3 = (f32[128,1024]{1,0:T(8,128)S(1)}, f32[128,1024]{1,0:T(8,128)}, u32[]{:S(2)}) copy-start(f32[128,1024]{1,0:T(8,128)} %param.27) | copy-start | bytes 1572868
  6.5 1.5 copy-start.15
  6.5 2.2 copy-start.19
  9.3 154.1 %copy-start.23 = (s32[32]{0:T(128)S(1)}, s32[32]{0:T(128)}, u32[]{:S(2)}) copy-start(s32[32]{0:T(128)} %param.24) | copy-start | bytes 388
  163.5 3.7 copy-start.4
  571.6 2.0 copy-start.10
  571.6 2.0 copy-start.11
  573.6 1.4 copy-start.2
  573.6 1.9 copy-start.7
  573.6 2.2 copy-start.8
  573.6 2.4 copy-start.9
  576.0 1.8 copy-start.16
  576.0 1.8 copy-start.17
  576.0 1.8 copy-start.18
  576.0 2.6 copy-start.20
  576.0 2.6 copy-start.21
  576.0 2.6 copy-start.22
  576.0 3.2 copy-start.12
  576.1 3.2 copy-start.13
  576.1 3.2 copy-start.14
  578.6 2.0 copy-start.6
  580.6 2.3 copy-start.5
  580.6 3.7 copy-start.1

commit v2 on v1

--- a/solution.py
+++ b/solution.py
@@ -83,6 +83,18 @@
     def z_off(self, i):
         return lax.rem(self.z + i, self.nz)
 
+    def z_flip(self, bit):
+        return self.z + bit - 2 * bit * lax.rem(lax.div(self.z, bit), 2)
+
+    def z_mask(self, mask):
+        out = self.z
+        bit = 1
+        while bit < self.nz:
+            if mask & bit:
+                out = out + bit - 2 * bit * lax.rem(lax.div(self.z, bit), 2)
+            bit *= 2
+        return out
+
     def neighbours(self):
         out = [self.at(a=1 - self.a), self.at(c=1 - self.c)]
         out += [self.at(b=self.b_off(i)) for i in range(1, self.nb)]
@@ -129,6 +141,12 @@
         copy.wait_send()
 
 
+def add_all(terms):
+    if len(terms) == 2:
+        return terms[0] + terms[1]
+    return sum(t.astype(F32) for t in terms).astype(terms[0].dtype)
+
+
 def gather_copies(nb, nz):
     return (nz - 1) + 1 + (nb - 1) + (nb - 1) + 1 + 1
 
@@ -140,11 +158,11 @@
         half = rows // 2
         own = pl.ds(pl.multiple_of(z * width, LANES), width)
         top, low = pl.ds(0, half), pl.ds(half, half)
-        shard = src
         mine = out.at[a, b, c, :, own]
-        self.local = pltpu.make_async_copy(shard, mine, local_sem)
-        self.phases = [
-            [sems.copy(shard, mine, spot.at(z=spot.z_off(i))) for i in range(1, spot.nz)],
+        self.local = pltpu.make_async_copy(src, mine, local_sem)
+        self.phases = [[sems.copy(src, mine, spot.at(z=spot.z_off(i))) for i in range(1, spot.nz)]]
+        self.along = len(self.phases)
+        self.phases += [
             [sems.copy(out.at[a, b, c, top], out.at[a, b, c, top], spot.at(a=1 - a))]
             + [
                 sems.copy(out.at[a, b, c, low], out.at[a, b, c, low], spot.at(b=spot.b_off(i)))
@@ -161,7 +179,7 @@
     def start(self, p):
         if p == 0:
             self.local.start()
-        if p == 1:
+        if p == self.along:
             self.local.wait()
         start_all(self.phases[p])
 
@@ -197,11 +215,11 @@
         send_done(self.copies)
 
 
-def timeline(pieces, times, which=(0, 1, 2, 3, 4)):
+def timeline(pieces, times):
     phases = len(pieces[0].phases)
     steps = {}
     for t in reversed(range(len(pieces))):
-        for p in which:
+        for p in range(phases + 1):
             steps.setdefault(times[t][p], []).append((t, p))
 
     def run(events):
@@ -247,13 +265,6 @@
         return carry
 
     lax.fori_loop(0, span // ROWS, step, 0)
-
-
-def slot_times(slot, count):
-    return [
-        [0 if t == 0 else slot(t - 1) + 1, slot(t), slot(t + 1) + 1, slot(t + 2) + 2, slot(t + 3) + 3]
-        for t in range(count)
-    ]
 
 
 def reduce_copies(nb, nz):
@@ -272,7 +283,6 @@
         top, low = pl.ds(0, half), pl.ds(half, half)
         self.local = None if src is None else pltpu.make_async_copy(src.at[:, :, c], acc, local_sem)
         columns = lambda zz: pl.ds(pl.multiple_of(zz * self.width, LANES), self.width)
-        self.own_columns = columns(z)
         self.phases = [
             [sems.copy(other, self.r0, spot.at(c=1 - c))],
             [
@@ -285,13 +295,22 @@
                 sems.copy(acc.at[a, spot.b_off(i), low], self.r2b.at[i - 1], spot.at(b=spot.b_off(i)))
                 for i in range(1, spot.nb)
             ],
-            [
-                sems.copy(
-                    acc.at[a, b, :, columns(spot.z_off(i))], self.r3.at[i - 1], spot.at(z=spot.z_off(i))
-                )
-                for i in range(1, spot.nz)
-            ],
         ]
+        self.columns = columns
+        self.landed = []
+        bit, slot = 1, 0
+        while bit < spot.nz:
+            masks = [m for m in range(spot.nz) if m & bit and m % bit == 0]
+            target = spot.at(z=spot.z_flip(bit))
+            self.phases.append(
+                [
+                    sems.copy(acc.at[a, b, :, columns(spot.z_mask(m))], self.r3.at[slot + i], target)
+                    for i, m in enumerate(masks)
+                ]
+            )
+            self.landed.append([(m ^ bit, slot + i) for i, m in enumerate(masks)])
+            slot += len(masks)
+            bit *= 2
 
     def start(self, p):
         if p == 0 and self.local is not None:
@@ -308,26 +327,22 @@
                 self.local.wait()
             for i in range(2):
                 for j in range(spot.nb):
-                    acc[i, j] = (acc[i, j].astype(F32) + self.r0[i, j].astype(F32)).astype(BF)
+                    acc[i, j] = acc[i, j] + self.r0[i, j]
         if p == 1:
             for i in range(2):
-                total = acc[i, b, top].astype(F32)
-                for k in range(spot.nb - 1):
-                    total = total + self.r1b[k, i].astype(F32)
-                acc[i, b, top] = total.astype(BF)
+                acc[i, b, top] = add_all([acc[i, b, top]] + [self.r1b[k, i] for k in range(spot.nb - 1)])
             for j in range(spot.nb):
-                acc[a, j, low] = (acc[a, j, low].astype(F32) + self.r1a[j].astype(F32)).astype(BF)
+                acc[a, j, low] = acc[a, j, low] + self.r1a[j]
         if p == 2:
-            acc[a, b, top] = (acc[a, b, top].astype(F32) + self.r2a[...].astype(F32)).astype(BF)
-            total = acc[a, b, low].astype(F32)
-            for k in range(spot.nb - 1):
-                total = total + self.r2b[k].astype(F32)
-            acc[a, b, low] = total.astype(BF)
-        if p == 3:
-            total = acc[a, b, :, self.own_columns].astype(F32)
-            for k in range(spot.nz - 1):
-                total = total + self.r3[k].astype(F32)
-            self.finish(total)
+            acc[a, b, top] = acc[a, b, top] + self.r2a[...]
+            acc[a, b, low] = add_all([acc[a, b, low]] + [self.r2b[k] for k in range(spot.nb - 1)])
+        if p >= 3:
+            for mask, slot in self.landed[p - 3]:
+                block = self.columns(spot.z_mask(mask))
+                if p == len(self.phases) - 1:
+                    self.finish(acc[a, b, :, block].astype(F32) + self.r3[slot].astype(F32))
+                else:
+                    acc[a, b, :, block] = acc[a, b, :, block] + self.r3[slot]
 
     def close(self):
         for phase in self.phases:
@@ -529,14 +544,14 @@
     return [(lax.div(i, spot.nz), lax.rem(i, spot.nz)) for i in ids]
 
 
-def project_and_attend(mesh, low_in, low_rest, low_vectors, sequence, place, marks, parts):
+def project_and_attend(mesh, low_in, low_rest, low_vectors, sequence, places, lengths, parts):
     groups, depth = mesh.shape["grp"], mesh.shape["dp"]
     nb = groups // 4
     count, block, width = low_in.shape
     rest = low_rest.shape[0]
     span, columns = sequence.shape
     devices = groups * depth
-    few = place.shape[1]
+    few = places.shape[1]
     pairs = H // 2
     total = (count + rest) * gather_copies(nb, depth) + depth - 1 + devices - 1
     lag = 3
@@ -550,8 +565,9 @@
     def slot(s):
         return 4 * s if s < attend else 4 * attend + 6 * (s - attend)
 
-    def kernel(in_ref, rest_ref, vec_ref, seq_ref, place_ref, marks_ref, part_ref,
+    def kernel(in_ref, rest_ref, vec_ref, seq_ref, places_ref, lengths_ref, part_ref,
                full_ref, out_ref, up_ref, vec_full_ref, proj_ref, few_ref, a_ref, lse_ref, lse_global_ref, swapped_ref,
+               marks_ref, place_ref, vec_out_ref,
                weight, vec, proj, bias, send, recv, local):
         spot = Spot(groups, depth)
         sems = Sems(send, recv)
@@ -568,9 +584,12 @@
         ]
         step = pl.program_id(0)
         ticks = Ticks(4)
-        times = slot_times(slot, count + rest)
-        for t in range(local_count, count + rest):
-            times[t] = [slot(t - 2) + 1, slot(t), slot(t + 2) + 1, slot(t + 4) + 2, slot(t + 5) + 3]
+        times = []
+        for t in range(count + rest):
+            if t < local_count:
+                times.append([max(0, slot(t - 1) + 1), slot(t), slot(t + 1) + 1, slot(t + 2) + 2, slot(t + 3) + 3])
+            else:
+                times.append([slot(t - 2) + 1, slot(t), slot(t + 2) + 1, slot(t + 4) + 2, slot(t + 5) + 3])
         ticks.add_all(timeline(pieces, times))
         for j in range(8):
             ticks.add(4 * (attend + 2 * j if j < 4 else project + j - 4) + 2, lambda j=j: swap.start(j, 8))
@@ -586,6 +605,17 @@
 
         @pl.when(step == 0)
         def _():
+            me = spot.g * depth + spot.z
+            spots = places_ref[pl.ds(me, 1), :]
+            length = lengths_ref[pl.ds(me, 1), :]
+            for i in range(0, span, ROWS):
+                hit = (lax.broadcasted_iota(jnp.int32, (ROWS, few), 0) + i == spots).astype(F32)
+                if i == 0:
+                    place_ref[...] = hit.astype(BF)
+                is_global = jnp.max(hit, axis=1, keepdims=True)
+                lane = lax.broadcasted_iota(jnp.int32, (ROWS, LANES), 1)
+                valid = (lax.broadcasted_iota(jnp.int32, (ROWS, LANES), 0) + i < length).astype(F32)
+                marks_ref[i : i + ROWS, :] = jnp.where(lane == 0, valid, jnp.where(lane == 1, is_global, 0.0))
             make_bias(marks_ref, bias)
 
         @pl.when(step == lag)
@@ -594,6 +624,7 @@
             recv_all(vec_sends)
             send_done(vec_sends)
             pltpu.sync_copy(vec_full_ref, vec)
+            vec_out_ref[...] = vec[...].astype(F32)
 
         def offset(row):
             index = lax.broadcasted_iota(jnp.int32, vec.shape, 0)
@@ -658,7 +689,7 @@
     results = pl.pallas_call(
         kernel,
         grid=(steps,),
-        in_specs=[ANYSPEC] * 3 + [still(span, columns), still(*place.shape), still(*marks.shape), ANYSPEC],
+        in_specs=[ANYSPEC] * 3 + [still(span, columns), still(*places.shape), still(*lengths.shape), ANYSPEC],
         out_specs=[ANYSPEC] * 5
         + [
             pl.BlockSpec((few, columns), lambda s: (0, 0)),
@@ -666,6 +697,9 @@
             pl.BlockSpec((1, 8, span), lambda s: (at(s), 0, 0)),
             pl.BlockSpec((pairs, 8, LANES), lambda s: (0, 0, 0)),
             ANYSPEC,
+            pl.BlockSpec((span, LANES), lambda s: (0, 0)),
+            pl.BlockSpec((ROWS, few), lambda s: (0, 0)),
+            pl.BlockSpec((low_vectors.shape[0], columns), lambda s: (0, 0)),
         ],
         out_shape=[
             jax.ShapeDtypeStruct(full_shape(nb, block, columns, count), BF),
@@ -678,6 +712,9 @@
             jax.ShapeDtypeStruct((pairs, 8, span), F32),
             jax.ShapeDtypeStruct((pairs, 8, LANES), F32),
             jax.ShapeDtypeStruct(parts.shape, BF),
+            jax.ShapeDtypeStruct((span, LANES), F32),
+            jax.ShapeDtypeStruct((ROWS, few), BF),
+            jax.ShapeDtypeStruct((low_vectors.shape[0], columns), F32),
         ],
         scratch_shapes=[
             pltpu.VMEM(full_shape(nb, block, columns), BF),
@@ -690,7 +727,7 @@
         ],
         compiler_params=kernel_params(0),
         name="project_and_attend",
-    )(low_in, low_rest, low_vectors, sequence, place, marks, parts)
+    )(low_in, low_rest, low_vectors, sequence, places, lengths, parts)
     square = (groups * block, columns)
     full_in, full_out, full_up = results[:3]
     return (full_in.reshape((count,) + square), full_out.reshape(square), full_up.reshape((rest - 1,) + square)) + tuple(
@@ -729,7 +766,7 @@
 
         ticks = Ticks(8)
         starts = [[0, 1, 2, 3], [8, 16, 24, 32], [10, 19, 28, 37], [18, 27, 36, 45], [25, 34, 44, 52]]
-        ticks.add_all(timeline(pieces, [[starts[p][q] for p in range(5)] for q in range(count)]))
+        ticks.add_all(timeline(pieces, [[row[q] for row in starts] for q in range(count)]))
         for j, tick in enumerate((3, 5, 8, 9, 10, 11, 16, 17)):
             ticks.add(tick, lambda j=j: swap.start(j, 8))
         chunks = [slice(i, i + ROWS) for i in range(0, span, ROWS)]
@@ -897,8 +934,9 @@
         fetch = pltpu.make_async_copy(sum_ref, norm, local.at[2])
         step = pl.program_id(0)
         ticks = Ticks(4)
-        starts = [[3, 7, 11, 15], [7, 19, 27, 35], [17, 25, 33, 41], [22, 30, 38, 46], [31, 39, 47, 53]]
-        ticks.add_all(timeline(pieces, [[starts[p][q] for p in range(5)] for q in range(count)]))
+        starts = [[3, 7, 11, 15], [7, 19, 27, 35], [17, 25, 33, 41], [22, 30, 38, 46]]
+        starts += [[26, 34, 42, 50]] * (len(pieces[0].phases) - 4) + [[31, 39, 47, 54]]
+        ticks.add_all(timeline(pieces, [[row[q] for row in starts] for q in range(count)]))
         for j in range(8):
             ticks.add(4 * (j + 2), lambda j=j: swap.start(j, 8))
         chunks = [slice(i, i + ROWS) for i in range(0, span, ROWS)]
@@ -950,7 +988,7 @@
             def body(rows):
                 adjoint = norm[rows, :]
                 centered = normal_ref[rows, :].astype(F32)
-                back = normalize_back(adjoint, centered, spread_ref[rows, 0:1], gain_ref[0:1, :])
+                back = normalize_back(adjoint, centered, spread_ref[rows, 0:1], gain_ref[6 + count : 7 + count, :])
                 back_branch = back.astype(BF)
                 norm[rows, :] = back
                 branch[rows, :] = back_branch
@@ -984,7 +1022,7 @@
             by_half, by_half,
             pl.BlockSpec((1, half, columns), lambda s: (lax.div(at(s), 2), lax.rem(at(s), 2), 0)),
             ANYSPEC, still(span, columns), still(columns, columns), still(span, columns), still(span, LANES),
-            still(8, columns), ANYSPEC,
+            still(*gain.shape), ANYSPEC,
         ],
         out_specs=[
             by_half,
@@ -1032,10 +1070,12 @@
     vec_rows = 16
     extra = hidden_sums.shape[0]
     total = (early + count) * reduce_copies(nb, depth) + devices - 1 + depth - 1 + groups - 1
-    late_starts = [4 * (pairs + t) + 3 for t in range(count)]
-    late_times = [[m, m + 3, m + 9, m + 12, m + 16] for m in late_starts]
-    steps = late_times[-1][-1] // 4 + 1
-    boxes = [reduce_boxes(nb, depth, block, columns) for _ in range(max(early + 1, count))]
+    late_starts = [4 * (pairs + t) + 1 for t in range(count)]
+    fresh = early - early // 2
+    steps = (late_starts[-1] + 17) // 4 + 1
+    boxes = [reduce_boxes(nb, depth, block, columns) for _ in range(early + fresh)]
+    for i in range(count - fresh, early):
+        boxes[i][0] = pltpu.VMEM((2, nb, 1, block, columns), BF)
     per = len(boxes[0])
 
     def kernel(*refs):
@@ -1060,7 +1100,7 @@
             ReducePiece(spot, sems, local.at[i], change_refs[v].at[t], width, box(i), finish(own_refs[v], t))
             for i, (v, t) in enumerate(where)
         ]
-        late_box = [early] + list(range(early)) + list(range(early + 1, count))
+        late_box = list(range(early, early + fresh)) + list(range(count - fresh))
         late = [
             ReducePiece(spot, sems, None, None, width, box(late_box[t]), finish(own_in_ref, int(order[t]))) for t in range(count)
         ]
@@ -1079,18 +1119,26 @@
         ]
         step = pl.program_id(0)
         ticks = Ticks(4)
+        more = len(pieces[0].phases) - 4
         ticks.add_all(
-            timeline(pieces, [[max(0, 5 * t - 3), 5 * t + 2, 5 * t + 6, 5 * t + 9, 5 * t + 13] for t in range(early)])
+            timeline(
+                pieces,
+                [
+                    [max(0, 6 * t - 4), 6 * t + 2, 6 * t + 10, 6 * t + 18] + [6 * t + 21] * more + [6 * t + 25]
+                    for t in range(early)
+                ],
+            )
         )
-        for j, tick in enumerate((1, 5, 9, 13, 17, 29, 32, 35)):
-            ticks.add(tick, lambda j=j: swap.start(j, 8))
+        for j in range(4 * pairs - 1):
+            ticks.add(1 + j, lambda j=j: swap.start(j, 4 * pairs - 1))
 
         def freed():
             for target in spot.neighbours():
                 pl.semaphore_signal(free, inc=1, device_id=target, device_id_type=MESH)
 
-        ticks.add(5 * (early - 1) + 13, freed)
-        ticks.add(late_starts[1], lambda: pl.semaphore_wait(free, len(spot.neighbours())))
+        ticks.add(6 * (count - fresh - 1) + 25, freed)
+        ticks.add(late_starts[fresh], lambda: pl.semaphore_wait(free, len(spot.neighbours())))
+        late_times = [[m, m + 2, m + 7, m + 12] + [m + 14] * more + [m + 17] for m in late_starts]
         ticks.add_all(timeline(late, late_times))
 
         @pl.when(step == 0)
@@ -1123,7 +1171,6 @@
             start_all(first)
 
         ticks.here(0, pairs, steps - 1)
-        ticks.here(1, pairs, steps - 1)
 
         for t in range(count - 1):
 
@@ -1132,18 +1179,27 @@
                 value = product_left(seq_ref[...], back[t]).astype(BF)
                 tiles[t][...] = value.reshape(full_shape(nb, block, columns))
 
-        @during(pairs, pairs + count - 2)
-        def _():
-            def body(rows):
-                grad[rows, :] += product_back(back[step - pairs, rows, :], weight_ref[0])
-
-            in_chunks(span, body)
-
         @pl.when(step == pairs + count - 1)
         def _():
             rows = product_left(place_ref[...], seq_ref[:ROWS, :]).astype(BF)
             value = product_left(rows, dqg[...]).astype(BF)
             tiles[count - 1][...] = value.reshape(full_shape(nb, block, columns))
+
+        ticks.here(1, pairs, steps - 1)
+
+        def grad_rows(first_row, last_row):
+            @during(pairs, pairs + count - 2)
+            def _():
+                for r in range(first_row, last_row, ROWS):
+                    rows = slice(r, r + ROWS)
+                    grad[rows, :] += product_back(back[step - pairs, rows, :], weight_ref[0])
+
+        grad_rows(0, span // 2)
+        ticks.here(2, pairs, steps - 1)
+        grad_rows(span // 2, span)
+
+        @pl.when(step == pairs + count - 1)
+        def _():
             extra = product_back(dqg[...], weight_ref[0])
             grad[:ROWS, :] += lax.dot_general(
                 place_ref[...].astype(F32), extra, (((1,), (0,)), ((), ())),
@@ -1152,7 +1208,6 @@
             back[0] = grad[...].astype(BF)
             keep.start()
 
-        ticks.here(2, pairs, steps - 1)
         ticks.here(3, pairs, steps - 1)
 
         @pl.when(step == pairs + 1)
@@ -1190,7 +1245,9 @@
         ]
         + [ANYSPEC] * (given + 1)
         + [
-            pl.BlockSpec((1, columns, columns), lambda s: (jnp.clip(s - pairs, 0, count - 1), 0, 0)),
+            pl.BlockSpec(
+                (1, columns, columns), lambda s: (jnp.clip(s - pairs, 0, count - 1), 0, 0), pipeline_mode=pl.Buffered(1)
+            ),
             still(span, columns), ANYSPEC, still(*hidden_sums.shape), still(*feed_sums.shape), still(*norm_sums.shape),
         ],
         out_specs=[whole(v.shape[0], block, width) for v in views]
@@ -1245,11 +1302,8 @@
     devices = groups * depth
     span = tokens.shape[1]
     quarters = FF // D
-    me = lax.axis_index(("grp", "dp"))
     ids = jnp.arange(devices, dtype=jnp.int32)
     inverse = jnp.sum(jnp.where(deal[None, :] == ids[:, None], ids[None, :], 0), axis=1)
-    length = lengths[me]
-    spots = places[me]
     sequence = tokens[0]
     order = np.array([1, 2, 0, 4, 5, 3])
 
@@ -1259,27 +1313,20 @@
     nv = vectors.shape[0]
     low_vectors = jnp.pad(vectors, ((0, 16 - nv), (0, 0))).astype(BF)
 
-    positions = jnp.arange(span, dtype=jnp.int32)
-    is_global = jnp.any(positions[:, None] == spots[None, :], axis=1)
-    lane = jnp.arange(LANES)[None, :]
-    marks = jnp.where(lane == 0, (positions < length)[:, None], (lane == 1) & is_global[:, None]).astype(F32)
-    place = (positions[:ROWS, None] == spots[None, :]).astype(BF)
     shape_parts = (devices, span // devices, D)
 
-    (full_in, full_out, full_up, full_vectors, projected, query_global, attended, log_sums, log_sums_global,
-     cotangent_parts) = project_and_attend(
-        mesh, low_in, low_rest, low_vectors, sequence, place, marks, out_cotangent.reshape(shape_parts)
+    (full_in, full_out, full_up, _, projected, query_global, attended, log_sums, log_sums_global,
+     cotangent_parts, marks, place, vector_rows) = project_and_attend(
+        mesh, low_in, low_rest, low_vectors, sequence, places, lengths[:, None], out_cotangent.reshape(shape_parts)
     )
-    vector_rows = full_vectors.astype(F32)
     hidden_bias = vector_rows[5 : 5 + quarters].reshape(groups, quarters, -1).transpose(1, 0, 2).reshape(quarters, D)
     cotangent_parts = cotangent_parts.at[deal].get(mode="promise_in_bounds")
     full_down, hidden, slope, first_low, normal_one, spread_one, layer_out, feed_low, sum_adjoint, feed_sums = feed_forward(
         mesh, sequence, attended, full_out, full_up, low_down, cotangent_parts, vector_rows, hidden_bias, marks
     )
-    gain_one = jnp.broadcast_to(vector_rows[6 + quarters][None], (8, D))
     up_change, hidden_sums, mixture_adjoint, part_down, layer_parts, out_change, attended_adjoint, norm_sums = feed_backward(
         mesh, feed_low, first_low, hidden, slope, full_up, full_down, sum_adjoint, attended, full_out, normal_one, spread_one,
-        gain_one, layer_out.reshape(shape_parts)
+        vector_rows, layer_out.reshape(shape_parts)
     )
     layer_parts = layer_parts.at[inverse].get(mode="promise_in_bounds")
     hidden_bias_change = hidden_sums[:, 0].reshape(quarters, groups, -1).transpose(1, 0, 2).reshape(quarters, D)

time: 593 us -> 559 us (0.943)
  Pallas kernels: 548 us -> 521 us
    pallas_call x1, Pallas kernels: 183 us -> 169 us  [attend_back_and_reduce(): pl.pallas_call(kernel, grid=(steps,), in_specs=[pl.BlockSpec((5, span, LA...]
    pallas_call x1, Pallas kernels: 117 us -> 104 us  [feed_backward(): pl.pallas_call(kernel, grid=(steps,), in_specs=[still(span, columns), sti...]
where the time goes in v2:
time: 559 us; the launch traced here: 551 us
  Pallas kernels  521 us (93%)
  local copies, waits for them, and re-layouts  17.8 us (3%)
  other arithmetic  10.8 us (2%)
    pallas_call x1, Pallas kernels, attend_back_and_reduce(): pl.pallas_call(kernel, grid=(steps,), in_specs=[pl.BlockSpec((5, span, LA...  169 us
    pallas_call x1, Pallas kernels, project_and_attend(): pl.pallas_call(kernel, grid=(steps,), in_specs=[ANYSPEC] * 3 + [still(spa...  152 us
    pallas_call x1, Pallas kernels, feed_backward(): pl.pallas_call(kernel, grid=(steps,), in_specs=[still(span, columns), sti...  104 us
    pallas_call x1, Pallas kernels, feed_forward(): pl.pallas_call(kernel, grid=(steps,), in_specs=[still(span, columns), sti...  96.9 us

profile of v2, /device:TPU:0, one launch (start us, length us, event | category | flops | bytes accessed | tf_op | source)
XLA Modules:
  0.0 551.1 jit_solution(3982690061949442845)
XLA Ops:
  0.7 1.2 convert.14
  1.9 0.0 copy-start.12
  2.0 0.8 pad_maximum_fusion.in_ref
  2.8 0.2 reshape.102
  3.0 0.2 copy.52
  3.2 0.2 reshape.103
  3.4 0.8 pad_maximum_fusion.1.rest_ref
  4.2 0.7 copy.43.lengths_ref
  4.9 0.6 pad.5.vec_ref
  5.5 151.5 %project_and_attend.1 = (bf16[6,2,2,2,128,1024]{5,4,3,2,1,0:T(8,128)(2,1)}, bf16[2,2,2,128,1024]{4,3,2,1,0:T(8,128)(2,1)}, bf16[4,2,2,2,128,1024]{5,4,3,2,1,0:T(...) custom-call(bf16[6,128,256]{2,1,0:T(8,128)(2,1)} %pad_maximum_fusion, ...), custom_call_target="tpu_custom_call" | custom-call | tf_op jit(solution)/shard_map/project_and_attend/pallas_call | solution.py:689
  157.0 0.8 slice.33
  157.9 0.6 copy.53
  158.5 3.6 gather_fusion
  162.2 0.7 convert_element_type.15
  162.9 96.9 %feed_forward.1 = (bf16[4,2,2,2,128,1024]{5,4,3,2,1,0:T(8,128)(2,1)}, bf16[4,1024,1024]{2,1,0:T(8,128)(2,1)}, bf16[4,1024,1024]{2,1,0:T(8,128)(2,1)}, bf16[1024,...) custom-call(bf16[1024,1024]{1,0:T(8,128)(2,1)} %bitcast.51, ...), custom_call_target="tpu_custom_call" | custom-call | tf_op jit(solution)/shard_map/feed_forward/pallas_call | solution.py:866
  259.9 104.2 %feed_backward.1 = (bf16[4,1024,1024]{2,1,0:T(8,128)(2,1)}, f32[4,8,1024]{2,1,0:T(8,128)}, f32[1024,1024]{1,0:T(8,128)}, f32[4,128,256]{2,1,0:T(8,128)}, bf16[32...) custom-call(bf16[1024,1024]{1,0:T(8,128)(2,1)} %get-tuple-element.62.feed_r, ...), custom_call_target="tpu_custom_call" | custom-call | tf_op jit(solution)/shard_map/feed_backward/pallas_call | solution.py:1016
  364.1 0.1 select_reduce_fusion
  364.2 3.6 gather_fusion.1
  367.8 0.9 slice.34
  368.7 0.6 reshape.115.refs_14_
  369.4 168.6 %attend_back_and_reduce.1 = (f32[4,128,256]{2,1,0:T(8,128)}, f32[1,128,256]{2,1,0:T(8,128)}, f32[6,128,256]{2,1,0:T(8,128)}, f32[16,256]{1,0:T(8,128)}, bf16[102...) custom-call(bf16[5,1024,1024]{2,1,0:T(8,128)(2,1)} %get-tuple-element.53.refs_0_, ...), custom_call_target="tpu_custom_call" | custom-call | tf_op jit(solution)/shard_map/attend_back_and_reduce/pallas_call | solution.py:1237
  538.0 1.4 reshape.117
  539.4 0.3 copy.46
  539.7 0.2 reshape.118
  540.0 2.6 multiply_add_fusion.2
  542.7 1.7 multiply_add_fusion
  544.4 0.8 multiply_add_fusion.3
  545.2 0.6 multiply_add_fusion.4
  545.8 1.4 multiply_add_fusion.1
  547.2 1.3 copy.58
  548.5 1.0 copy-done.3
  549.5 1.3 copy.59
  (54 shorter events, 0.2 us)
Async XLA Ops:
  0.7 2.1 copy-start.1
  1.9 1.5 copy-start.12
  1.9 2.2 copy-start.20
  2.0 2.9 copy-start.16
  5.5 153.0 %copy-start.21 = (s32[32]{0:T(128)S(1)}, s32[32]{0:T(128)}, u32[]{:S(2)}) copy-start(s32[32]{0:T(128)} %param.24) | copy-start | bytes 388
  158.5 3.7 copy-start.2
  538.0 1.9 copy-start.8
  539.9 2.6 copy-start
  539.9 2.6 copy-start.5
  540.0 2.6 copy-start.6
  540.0 2.6 copy-start.7
  542.6 1.8 copy-start.13
  542.6 1.8 copy-start.14
  542.6 1.8 copy-start.15
  542.6 2.6 copy-start.17
  542.6 2.6 copy-start.18
  542.6 2.6 copy-start.19
  542.6 3.2 copy-start.9
  542.6 3.2 copy-start.10
  542.7 3.2 copy-start.11
  545.2 2.0 copy-start.4
  547.2 2.3 copy-start.3

commit v3 on v2

--- a/solution.py
+++ b/solution.py
@@ -28,7 +28,7 @@
 LANES = 128
 ROWS = 256
 ANYSPEC = pl.BlockSpec(memory_space=pl.ANY)
-VMEMSPEC = pl.BlockSpec(memory_space=pltpu.VMEM)
+SMEMSPEC = pl.BlockSpec(memory_space=pltpu.SMEM)
 
 
 def product(left_side, right_side):
@@ -213,6 +213,14 @@
         self.local.wait()
         recv_all(self.copies)
         send_done(self.copies)
+
+
+def reorder(index_ref, source, target):
+    def one(i, carry):
+        target[i] = source[index_ref[i]]
+        return carry
+
+    lax.fori_loop(0, target.shape[0], one, 0)
 
 
 def timeline(pieces, times):
@@ -735,7 +743,7 @@
     )
 
 
-def feed_forward(mesh, sequence, attended, full_out, full_up, shards, parts, vectors, hidden_bias, valid):
+def feed_forward(mesh, sequence, attended, full_out, full_up, shards, parts, index, vectors, hidden_bias, valid):
     groups, depth = mesh.shape["grp"], mesh.shape["dp"]
     nb = groups // 4
     span, columns = sequence.shape
@@ -745,13 +753,13 @@
     steps = count + 3
     extra = FF // D
 
-    def kernel(seq_ref, att_ref, wo_ref, up_ref, shard_ref, part_ref, vec_ref, hb_ref, valid_ref,
+    def kernel(seq_ref, att_ref, wo_ref, up_ref, shard_ref, part_ref, index_ref, vec_ref, hb_ref, valid_ref,
                full_ref, hid_ref, slope_ref, low_ref, normal_ref, spread_ref, layer_ref, feed_low_ref, sum_ref, sums_ref,
-               first, low, normal, hidden, feed, weight, cot, send, recv, local):
+               first, low, normal, hidden, feed, weight, dealt, cot, send, recv, local):
         spot = Spot(groups, depth)
         sems = Sems(send, recv)
         pieces = [GatherPiece(spot, sems, local.at[t], shard_ref.at[t], full_ref.at[t]) for t in range(count)]
-        swap = Swap(spot, sems, local.at[count], part_ref, cot)
+        swap = Swap(spot, sems, local.at[count], dealt, cot)
         keep_low = pltpu.make_async_copy(low, low_ref, local.at[count + 1])
         keep_normal = pltpu.make_async_copy(normal, normal_ref, local.at[count + 2])
         keep_hidden = [
@@ -763,6 +771,7 @@
         @pl.when(step == 0)
         def _():
             greet(everyone(spot))
+            reorder(index_ref, part_ref, dealt)
 
         ticks = Ticks(8)
         starts = [[0, 1, 2, 3], [8, 16, 24, 32], [10, 19, 28, 37], [18, 27, 36, 45], [25, 34, 44, 52]]
@@ -867,7 +876,7 @@
         kernel,
         grid=(steps,),
         in_specs=[
-            still(span, columns), still(span, columns), still(*full_out.shape), by_q, ANYSPEC, ANYSPEC,
+            still(span, columns), still(span, columns), still(*full_out.shape), by_q, ANYSPEC, still(*parts.shape), SMEMSPEC,
             still(*vectors.shape), still(*hidden_bias.shape), still(*valid.shape),
         ],
         out_specs=[ANYSPEC, ANYSPEC, by_q, ANYSPEC, ANYSPEC]
@@ -887,13 +896,14 @@
             pltpu.VMEM((span, columns), F32),
             pltpu.VMEM(full_shape(nb, block, columns), BF),
             pltpu.VMEM(parts.shape, BF),
+            pltpu.VMEM(parts.shape, BF),
             dma(total),
             dma(total),
             dma(2 * count + 4),
         ],
         compiler_params=kernel_params(1),
         name="feed_forward",
-    )(sequence, attended, full_out, full_up, shards, parts, vectors, hidden_bias, valid)
+    )(sequence, attended, full_out, full_up, shards, parts, index, vectors, hidden_bias, valid)
     return (results[0].reshape(count, groups * block, columns),) + tuple(results[1:])
 
 
@@ -1124,7 +1134,7 @@
             timeline(
                 pieces,
                 [
-                    [max(0, 6 * t - 4), 6 * t + 2, 6 * t + 10, 6 * t + 18] + [6 * t + 21] * more + [6 * t + 25]
+                    [max(0, 6 * t - 4), 6 * t + 2, 6 * t + 12, 6 * t + 22] + [6 * t + 26] * more + [6 * t + 30]
                     for t in range(early)
                 ],
             )
@@ -1136,7 +1146,7 @@
             for target in spot.neighbours():
                 pl.semaphore_signal(free, inc=1, device_id=target, device_id_type=MESH)
 
-        ticks.add(6 * (count - fresh - 1) + 25, freed)
+        ticks.add(6 * (count - fresh - 1) + 30, freed)
         ticks.add(late_starts[fresh], lambda: pl.semaphore_wait(free, len(spot.neighbours())))
         late_times = [[m, m + 2, m + 7, m + 12] + [m + 14] * more + [m + 17] for m in late_starts]
         ticks.add_all(timeline(late, late_times))
@@ -1320,9 +1330,8 @@
         mesh, low_in, low_rest, low_vectors, sequence, places, lengths[:, None], out_cotangent.reshape(shape_parts)
     )
     hidden_bias = vector_rows[5 : 5 + quarters].reshape(groups, quarters, -1).transpose(1, 0, 2).reshape(quarters, D)
-    cotangent_parts = cotangent_parts.at[deal].get(mode="promise_in_bounds")
     full_down, hidden, slope, first_low, normal_one, spread_one, layer_out, feed_low, sum_adjoint, feed_sums = feed_forward(
-        mesh, sequence, attended, full_out, full_up, low_down, cotangent_parts, vector_rows, hidden_bias, marks
+        mesh, sequence, attended, full_out, full_up, low_down, cotangent_parts, deal, vector_rows, hidden_bias, marks
     )
     up_change, hidden_sums, mixture_adjoint, part_down, layer_parts, out_change, attended_adjoint, norm_sums = feed_backward(
         mesh, feed_low, first_low, hidden, slope, full_up, full_down, sum_adjoint, attended, full_out, normal_one, spread_one,

time: 559 us -> 553 us (0.989)
  no operation moved by 1% of the time
where the time goes in v3:
time: 553 us; the launch traced here: 545 us
  Pallas kernels  519 us (94%)
  local copies, waits for them, and re-layouts  15.2 us (3%)
  other arithmetic  9.53 us (2%)
    pallas_call x1, Pallas kernels, attend_back_and_reduce(): pl.pallas_call(kernel, grid=(steps,), in_specs=[pl.BlockSpec((5, span, LA...  165 us
    pallas_call x1, Pallas kernels, project_and_attend(): pl.pallas_call(kernel, grid=(steps,), in_specs=[ANYSPEC] * 3 + [still(spa...  152 us
    pallas_call x1, Pallas kernels, feed_backward(): pl.pallas_call(kernel, grid=(steps,), in_specs=[still(span, columns), sti...  104 us
    pallas_call x1, Pallas kernels, feed_forward(): pl.pallas_call(kernel, grid=(steps,), in_specs=[still(span, columns), sti...  98.1 us

profile of v3, /device:TPU:0, one launch (start us, length us, event | category | flops | bytes accessed | tf_op | source)
XLA Modules:
  0.0 544.8 jit_solution(17105860077612927225)
XLA Ops:
  0.7 1.2 convert.14
  2.0 0.8 pad_maximum_fusion.in_ref
  2.8 0.2 reshape.102
  3.0 0.2 copy.52
  3.2 0.2 reshape.103
  3.4 0.8 pad_maximum_fusion.1.rest_ref
  4.2 0.7 copy.43.lengths_ref
  4.9 0.6 pad.5.vec_ref
  5.5 151.5 %project_and_attend.1 = (bf16[6,2,2,2,128,1024]{5,4,3,2,1,0:T(8,128)(2,1)}, bf16[2,2,2,128,1024]{4,3,2,1,0:T(8,128)(2,1)}, bf16[4,2,2,2,128,1024]{5,4,3,2,1,0:T(...) custom-call(bf16[6,128,256]{2,1,0:T(8,128)(2,1)} %pad_maximum_fusion, ...), custom_call_target="tpu_custom_call" | custom-call | tf_op jit(solution)/shard_map/project_and_attend/pallas_call | solution.py:697
  157.0 0.8 slice.33
  157.9 0.6 copy.53
  158.5 0.7 convert_element_type.15
  159.3 98.1 %feed_forward.1 = (bf16[4,2,2,2,128,1024]{5,4,3,2,1,0:T(8,128)(2,1)}, bf16[4,1024,1024]{2,1,0:T(8,128)(2,1)}, bf16[4,1024,1024]{2,1,0:T(8,128)(2,1)}, bf16[1024,...) custom-call(bf16[1024,1024]{1,0:T(8,128)(2,1)} %bitcast.51, ...), custom_call_target="tpu_custom_call" | custom-call | tf_op jit(solution)/shard_map/feed_forward/pallas_call | solution.py:875
  257.4 104.2 %feed_backward.1 = (bf16[4,1024,1024]{2,1,0:T(8,128)(2,1)}, f32[4,8,1024]{2,1,0:T(8,128)}, f32[1024,1024]{1,0:T(8,128)}, f32[4,128,256]{2,1,0:T(8,128)}, bf16[32...) custom-call(bf16[1024,1024]{1,0:T(8,128)(2,1)} %get-tuple-element.62.feed_r, ...), custom_call_target="tpu_custom_call" | custom-call | tf_op jit(solution)/shard_map/feed_backward/pallas_call | solution.py:1026
  361.8 3.6 gather_fusion
  365.4 0.9 slice.34
  366.3 0.6 reshape.115.refs_14_
  366.9 164.9 %attend_back_and_reduce.1 = (f32[4,128,256]{2,1,0:T(8,128)}, f32[1,128,256]{2,1,0:T(8,128)}, f32[6,128,256]{2,1,0:T(8,128)}, f32[16,256]{1,0:T(8,128)}, bf16[102...) custom-call(bf16[5,1024,1024]{2,1,0:T(8,128)(2,1)} %get-tuple-element.53.refs_0_, ...), custom_call_target="tpu_custom_call" | custom-call | tf_op jit(solution)/shard_map/attend_back_and_reduce/pallas_call | solution.py:1247
  531.9 1.4 reshape.117
  533.3 0.3 copy.46
  533.6 0.2 reshape.118
  533.9 1.4 multiply_add_fusion.2
  535.3 0.5 copy-done.5
  535.8 0.2 copy-done.6
  536.1 0.2 copy-done.7
  536.4 1.7 multiply_add_fusion
  538.1 0.8 multiply_add_fusion.3
  538.9 0.6 multiply_add_fusion.4
  539.5 1.4 multiply_add_fusion.1
  540.9 1.3 copy.58
  542.2 1.0 copy-done.3
  543.3 1.3 copy.59
  (53 shorter events, 0.3 us)
Async XLA Ops:
  0.7 2.1 copy-start.1
  1.9 1.5 copy-start.13
  1.9 2.2 copy-start.22
  2.0 2.9 copy-start.17
  5.5 153.0 %copy-start.2 = (f32[512,256]{1,0:T(8,128)S(1)}, f32[512,256]{1,0:T(8,128)}, u32[]{:S(2)}) copy-start(f32[512,256]{1,0:T(8,128)} %param.28) | copy-start | bytes 1572868
  257.4 104.3 %copy-start.21 = (s32[32]{0:T(128)S(1)}, s32[32]{0:T(128)}, u32[]{:S(2)}) copy-start(s32[32]{0:T(128)} %index_ref.1) | copy-start | bytes 388
  531.9 2.0 copy-start.8
  531.9 2.0 copy-start.9
  533.9 1.4 copy-start
  533.9 1.9 copy-start.5
  533.9 2.2 copy-start.6
  533.9 2.4 copy-start.7
  536.3 1.8 copy-start.14
  536.3 1.8 copy-start.15
  536.3 1.8 copy-start.16
  536.3 2.6 copy-start.18
  536.3 2.6 copy-start.19
  536.3 2.6 copy-start.20
  536.3 3.2 copy-start.10
  536.3 3.2 copy-start.11
  536.4 3.2 copy-start.12
  538.9 2.0 copy-start.4
  540.9 2.3 copy-start.3
